TPU v7x, 32 devices: a whole 2x2x4 slice. The times are simulated.
32 devices in a mesh: seq: 8 (over z, x), exp: 4 (over y, core).
Axes of the slice: x: 2, y: 2, z: 4, core: 2. Of those that a mesh axis runs over, the one named last changes fastest.
Arguments:
- tokens: bfloat16 [4096, 1536], P(('seq', 'exp')), may hold values from -6 to 6
- in_gain: float32 [1536], replicated, may hold values from 0.5 to 1.5
- in_z: bfloat16 [1536, 3072], P(None, 'exp'), may hold values from -0.15625 to 0.15625
- in_x: bfloat16 [1536, 3072], P(None, 'exp'), may hold values from -0.15625 to 0.15625
- in_bc: bfloat16 [1536, 256], replicated, may hold values from -0.15625 to 0.15625
- in_dt: bfloat16 [1536, 48], P(None, 'exp'), may hold values from -0.0390625 to 0.0390625
- conv_x: float32 [4, 3072], P(None, 'exp'), may hold values from -3 to 3
- conv_bc: float32 [4, 256], replicated, may hold values from -3 to 3
- dt_bias: float32 [48], P('exp'), may hold values from -7 to -2
- a_log: float32 [48], P('exp'), may hold values from -1 to 2.5
- d_skip: float32 [48], P('exp'), may hold values from 0.5 to 1.5
- norm_gain: float32 [3072], P('exp'), may hold values from 0.5 to 1.5
- out_w: bfloat16 [3072, 1536], P('exp'), may hold values from -0.109375 to 0.109375
- post_gain: float32 [1536], replicated, may hold values from 0.5 to 1.5
- sh_gate: bfloat16 [1536, 1024], P(None, 'exp'), may hold values from -0.15625 to 0.15625
- sh_up: bfloat16 [1536, 1024], P(None, 'exp'), may hold values from -0.15625 to 0.15625
- sh_down: bfloat16 [1024, 1536], P('exp'), may hold values from -0.1875 to 0.1875
- ex_gate: bfloat16 [32, 1536, 512], P('seq'), may hold values from -0.15625 to 0.15625
- ex_up: bfloat16 [32, 1536, 512], P('seq'), may hold values from -0.15625 to 0.15625
- ex_down: bfloat16 [32, 512, 1536], P('seq'), may hold values from -0.25 to 0.25
- routes: int32 [4096, 6], P(('seq', 'exp')), may hold values from 0 to 31, all different within a row; in each aligned block of 128 rows (0 to 127, 128 to 255, ...) at most 32 rows name the same one
- gates: float32 [4096, 6], P(('seq', 'exp')), may hold values from 0.1 to 1
- lengths: int32 [8], replicated, may hold values from 1 to 1024, 4096 in all
- cache_slot: int32 [8], replicated, may hold values from 0 to 7, each once
Outputs:
- layer_out: bfloat16 [4096, 1536], P(('seq', 'exp'))
- state_cache: float32 [8, 48, 64, 128], P('seq', 'exp')
Inputs may be any that keep to these rules, and one draw needn't show every extreme that they name: `routes`: in the rows of one device (aligned blocks of 128 rows) no expert is named by more than 32 rows, a bound that some block reaches; each row names 6 different experts. The lengths sum to 4096; the largest is exactly 1024. `cache_slot`: every slot is named once.
All inputs are finite; a program needn't handle non-finite values.
Results may differ from a plain program's by a relative error of at most 0.019.
Values may be sent and summed in bfloat16 or wider, within the bound.
A program may use at most 128 MiB of HBM per device.

v0:
```python
import jax
import jax.numpy as jnp
from jax import lax
from jax.sharding import PartitionSpec as P

BLOCK = 512
DI = 3072


epsilon = 1e-05
highest = lax.Precision.HIGHEST


def from_behind(block, axis, distance):
    devices = range(lax.axis_size(axis))
    route = [(i - distance, i) for i in devices if i - distance in devices]
    return lax.ppermute(block, axis, route)


def rms_rows(values, gain):
    meansq = jnp.mean(values * values, axis=-1, keepdims=True)
    return values * lax.rsqrt(meansq + epsilon) * gain


def segment_of(positions, req_ends):
    return jnp.sum((positions[:, None] >= req_ends[None, :]).astype(jnp.int32), axis=1)


def causal_conv(extended, weight, ext_segment, segment, row_count):
    summed = jnp.zeros((row_count, extended.shape[1]), jnp.float32)
    for tap in range(weight.shape[0]):
        window = extended[tap : tap + row_count].astype(jnp.float32)
        kept = (ext_segment[tap : tap + row_count] == segment)[:, None]
        summed = summed + jnp.where(kept, weight[tap] * window, 0.0)
    return jax.nn.silu(summed).astype(jnp.bfloat16)


def body(
    tokens,
    in_gain,
    in_z,
    in_x,
    in_bc,
    in_dt,
    conv_x,
    conv_bc,
    dt_bias,
    a_log,
    d_skip,
    norm_gain,
    out_w,
    post_gain,
    sh_gate,
    sh_up,
    sh_down,
    ex_gate,
    ex_up,
    ex_down,
    routes,
    gates,
    lengths,
    cache_slot,
):
    seq_count = lax.axis_size("seq")
    own_rows = tokens.shape[0]
    width = tokens.shape[1]
    state_size = in_bc.shape[1] // 2
    local_heads = a_log.shape[0]
    head_width = conv_x.shape[1] // local_heads
    taps = conv_x.shape[0]
    stream = lax.all_gather(tokens, "exp", axis=0, tiled=True)
    row_count = stream.shape[0]
    normed_in = rms_rows(stream.astype(jnp.float32), in_gain).astype(jnp.bfloat16)
    gate_raw = jnp.dot(normed_in, in_z, preferred_element_type=jnp.float32).astype(jnp.bfloat16)
    conv_in_x = jnp.dot(normed_in, in_x, preferred_element_type=jnp.float32).astype(jnp.bfloat16)
    conv_in_bc = jnp.dot(normed_in, in_bc, preferred_element_type=jnp.float32).astype(jnp.bfloat16)
    dt_raw = jnp.dot(normed_in, in_dt, preferred_element_type=jnp.float32).astype(jnp.bfloat16)
    req_ends = jnp.cumsum(lengths)
    req_count = lengths.shape[0]
    req_ids = jnp.arange(req_count, dtype=jnp.int32)
    end_pos = req_ends - 1
    stream_start = lax.axis_index("seq") * row_count
    local_idx = jnp.arange(row_count, dtype=jnp.int32)
    segment = segment_of(stream_start + local_idx, req_ends)
    before_dev = jnp.where(
        stream_start > 0, segment_of(jnp.reshape(stream_start - 1, (1,)), req_ends)[0], -1
    )
    x_cols = conv_in_x.shape[1]
    tail_rows = jnp.concatenate(
        [conv_in_x[row_count - (taps - 1) :], conv_in_bc[row_count - (taps - 1) :]], axis=1
    )
    edge_rows = from_behind(tail_rows, "seq", 1)
    ext_x = jnp.concatenate([edge_rows[:, :x_cols], conv_in_x])
    ext_bc = jnp.concatenate([edge_rows[:, x_cols:], conv_in_bc])
    ext_pos = stream_start - (taps - 1) + jnp.arange(row_count + taps - 1, dtype=jnp.int32)
    ext_segment = jnp.where(ext_pos >= 0, segment_of(ext_pos, req_ends), -1)
    conv_x_out = causal_conv(ext_x, conv_x, ext_segment, segment, row_count)
    conv_bc_out = causal_conv(ext_bc, conv_bc, ext_segment, segment, row_count)
    b_all = conv_bc_out[:, :state_size]
    c_all = conv_bc_out[:, state_size:]
    step_size = jax.nn.softplus(dt_raw.astype(jnp.float32) + dt_bias)
    log_decay = -step_size * jnp.exp(a_log)
    heads_x = conv_x_out.reshape(row_count, local_heads, head_width)

    def block_step(carried, block):
        state, end_acc = carried
        drive_x, b_rows, c_rows, decay_rows, step_rows, block_seg, before_seg, base = block
        length = block_seg.shape[0]
        cumulative = jnp.cumsum(decay_rows, axis=0)
        order = jnp.arange(length, dtype=jnp.int32)
        same = (block_seg[:, None] == block_seg[None, :]) & (order[:, None] >= order[None, :])
        log_gap = cumulative[:, None, :] - cumulative[None, :, :]
        decay = jnp.where(same[:, :, None], jnp.exp(jnp.where(same[:, :, None], log_gap, 0.0)), 0.0)
        scores = jnp.dot(c_rows, b_rows.T, preferred_element_type=jnp.float32)
        drive = drive_x.astype(jnp.float32) * step_rows[:, :, None]
        weights = scores[:, :, None] * decay
        outputs = jnp.einsum("tsh,shp->thp", weights, drive, precision=highest)
        c_float = c_rows.astype(jnp.float32)
        b_float = b_rows.astype(jnp.float32)
        entry = jnp.where((block_seg == before_seg)[:, None], jnp.exp(cumulative), 0.0)
        outputs = outputs + entry[:, :, None] * jnp.einsum(
            "tn,hpn->thp", c_float, state, precision=highest
        )
        last_seg = block_seg[length - 1]
        tail = jnp.where(
            (block_seg == last_seg)[:, None],
            jnp.exp(cumulative[length - 1][None, :] - cumulative),
            0.0,
        )
        persist = jnp.where(last_seg == before_seg, jnp.exp(cumulative[length - 1]), 0.0)
        new_state = persist[:, None, None] * state + jnp.einsum(
            "sh,shp,sn->hpn", tail, drive, b_float, precision=highest
        )
        local_end = end_pos - base
        inside = (local_end >= 0) & (local_end < length)

        def close_request(req, acc):
            end_row = jnp.clip(local_end[req], 0, length - 1)
            cum_end = cumulative[end_row]
            member = (block_seg == req)[:, None]
            end_weights = jnp.where(
                member, jnp.exp(jnp.where(member, cum_end[None, :] - cumulative, 0.0)), 0.0
            )
            fresh = jnp.einsum("sh,shp,sn->hpn", end_weights, drive, b_float, precision=highest)
            holding = jnp.where(req == before_seg, jnp.exp(cum_end), 0.0)
            value = jnp.where(inside[req], fresh + holding[:, None, None] * state, 0.0)
            return lax.dynamic_update_index_in_dim(acc, acc[req] + value, req, 0)

        end_acc = lax.fori_loop(block_seg[0], last_seg + 1, close_request, end_acc)
        return ((new_state, end_acc), outputs)

    block_count = row_count // BLOCK

    def blocked(values):
        return values.reshape((block_count, BLOCK) + values.shape[1:])

    before_rows = jnp.concatenate([jnp.reshape(before_dev, (1,)), segment[:-1]])
    block_base = stream_start + jnp.arange(block_count, dtype=jnp.int32) * BLOCK
    blocks = (
        blocked(heads_x),
        blocked(b_all),
        blocked(c_all),
        blocked(log_decay),
        blocked(step_size),
        blocked(segment),
        blocked(before_rows)[:, 0],
        block_base,
    )
    zero_state = jnp.zeros((local_heads, head_width, state_size), jnp.float32)
    zero_ends = jnp.zeros((req_count, local_heads, head_width, state_size), jnp.float32)
    (end_state, end_local), outputs = lax.scan(block_step, (zero_state, zero_ends), blocks)
    outputs = outputs.reshape(row_count, local_heads, head_width)
    cum_dev = jnp.cumsum(log_decay, axis=0)
    pass_decay = jnp.where(
        segment[row_count - 1] == before_dev, jnp.exp(cum_dev[row_count - 1]), 0.0
    )

    def hop(_, state):
        return from_behind(
            (pass_decay[:, None, None] * state + end_state).astype(jnp.bfloat16), "seq", 1
        ).astype(jnp.float32)

    state_in = lax.fori_loop(0, seq_count - 1, hop, zero_state)
    leading = jnp.where((segment == before_dev)[:, None], jnp.exp(cum_dev), 0.0)
    carried_in = jnp.einsum("tn,hpn->thp", c_all.astype(jnp.float32), state_in, precision=highest)
    mixed_y = (
        outputs
        + leading[:, :, None] * carried_in
        + d_skip[None, :, None] * heads_x.astype(jnp.float32)
    )
    dev_end = end_pos - stream_start
    on_dev = (dev_end >= 0) & (dev_end < row_count)
    end_row = jnp.clip(dev_end, 0, row_count - 1)
    holding = jnp.where((on_dev & (req_ids == before_dev))[:, None], jnp.exp(cum_dev[end_row]), 0.0)
    end_all = end_local + holding[:, :, None, None] * state_in[None]
    placed = jnp.zeros_like(end_all).at[cache_slot].set(end_all)
    state_cache = lax.psum_scatter(
        placed.astype(jnp.bfloat16), "seq", scatter_dimension=0, tiled=True
    ).astype(jnp.float32)
    gated_flat = mixed_y.reshape(row_count, local_heads * head_width) * jax.nn.silu(
        gate_raw.astype(jnp.float32)
    )
    square_part = jnp.sum(gated_flat * gated_flat, axis=1)
    square_sum = lax.psum(square_part, "exp")
    scaled = (gated_flat * lax.rsqrt(square_sum / DI + epsilon)[:, None] * norm_gain).astype(
        jnp.bfloat16
    )
    mix_term = jnp.dot(scaled, out_w, preferred_element_type=jnp.float32)
    mixer_out = lax.psum_scatter(
        mix_term.astype(jnp.bfloat16), "exp", scatter_dimension=0, tiled=True
    ).astype(jnp.float32)
    residual = tokens.astype(jnp.float32) + mixer_out
    normed = rms_rows(residual, post_gain).astype(jnp.bfloat16)
    normed_all = lax.all_gather(normed, "exp", axis=0, tiled=True)
    shared_hidden = (
        jax.nn.silu(jnp.dot(normed_all, sh_gate, preferred_element_type=jnp.float32))
        * jnp.dot(normed_all, sh_up, preferred_element_type=jnp.float32)
    ).astype(jnp.bfloat16)
    shared = lax.psum_scatter(
        jnp.dot(shared_hidden, sh_down, preferred_element_type=jnp.float32).astype(jnp.bfloat16),
        "exp",
        scatter_dimension=0,
        tiled=True,
    ).astype(jnp.float32)
    top_count = routes.shape[1]
    owned = ex_gate.shape[0]
    experts = owned * seq_count
    capacity = own_rows * top_count * 4 // (3 * experts)
    flat_routes = routes.reshape(-1)
    onehot = (flat_routes[:, None] == jnp.arange(experts, dtype=jnp.int32)[None, :]).astype(
        jnp.int32
    )
    slot_rank = jnp.sum(onehot * (jnp.cumsum(onehot, axis=0) - 1), axis=1)
    slot_idx = flat_routes * capacity + slot_rank
    owner_tok = jnp.arange(own_rows * top_count, dtype=jnp.int32) // top_count
    slot_tok = jnp.full((experts * capacity,), own_rows, jnp.int32).at[slot_idx].set(owner_tok)
    padded = jnp.concatenate([normed, jnp.zeros((1, width), jnp.bfloat16)])
    outgoing = padded[slot_tok].reshape(seq_count, owned, capacity, width)
    received = lax.all_to_all(outgoing, "seq", split_axis=0, concat_axis=0, tiled=True)
    gate_part = jnp.einsum("secd,edf->secf", received, ex_gate, preferred_element_type=jnp.float32)
    up_part = jnp.einsum("secd,edf->secf", received, ex_up, preferred_element_type=jnp.float32)
    hidden = (jax.nn.silu(gate_part) * up_part).astype(jnp.bfloat16)
    expert_out = jnp.einsum(
        "secf,efd->secd", hidden, ex_down, preferred_element_type=jnp.float32
    ).astype(jnp.bfloat16)
    returned = lax.all_to_all(expert_out, "seq", split_axis=0, concat_axis=0, tiled=True)
    picked = returned.reshape(experts * capacity, width)[slot_idx].reshape(
        own_rows, top_count, width
    )
    routed = jnp.sum(gates[:, :, None] * picked.astype(jnp.float32), axis=1)
    layer_out = (residual + shared + routed).astype(jnp.bfloat16)
    return (layer_out, state_cache)


def solution(mesh):
    placed = (
        P(("seq", "exp"), None),
        P(),
        P(None, "exp"),
        P(None, "exp"),
        P(),
        P(None, "exp"),
        P(None, "exp"),
        P(),
        P("exp"),
        P("exp"),
        P("exp"),
        P("exp"),
        P("exp", None),
        P(),
        P(None, "exp"),
        P(None, "exp"),
        P("exp", None),
        P("seq", None, None),
        P("seq", None, None),
        P("seq", None, None),
        P(("seq", "exp"), None),
        P(("seq", "exp"), None),
        P(),
        P(),
    )
    return jax.shard_map(
        body,
        mesh=mesh,
        in_specs=placed,
        out_specs=(P(("seq", "exp"), None), P("seq", "exp", None, None)),
        check_vma=False,
    )
```

profile of v0, /device:TPU:0, one launch (start us, length us, event | category | flops | bytes accessed | tf_op | source)
XLA Modules:
  0.0 402.5 jit_solution(6934379756981183387)
XLA Ops:
  8.8 1.2 fusion.124
  15.4 1.4 fusion.134
  16.8 1.8 broadcast_compare_fusion.3
  19.6 12.4 %all-gather.3.cloned.1.call-done = bf16[512,1536]{1,0:T(8,128)(2,1)} async-done(((bf16[128,1536]{1,0:T(8,128)(2,1)}), bf16[512,1536]{1,0:T(8,128)(2,1)}) %all-gather.3.cloned.1.call-update) | async-done | bytes 1572880 | tf_op jit(solution)/shard_map/all_gather | solution.py:71
  32.0 1.9 fusion.46
  33.9 3.2 convolution_convert_fusion.3
  38.0 3.5 collective-permute-start.1
  42.3 1.2 reduce-window.21
  44.6 1.6 multiply_convert_fusion.4
  46.3 1.9 fusion.90
  48.2 1.3 fusion.101
  49.6 2.5 fusion.81
  52.1 3.0 copy.65
  55.1 2.3 fusion.69
  57.4 58.8 %while.32 = (s32[]{:T(128)}, f32[12,64,128]{2,1,0:T(8,128)S(1)}, f32[12]{0:T(128)S(1)}, f32[12,64,128]{2,1,0:T(8,128)S(1)}, s32[]{:T(128)}, /*index=5*/s32[]{:T(128)}) while((s32[]{:T(128)}, f32[12,64,128]{2,1,0:T(8,128)S(1)}, f32[12]{0:T(128)S(1)}, f32[12,64,128]{2,1,0:T(8,128)S(1)}, s32[]{:T(128)}, /*index=5*/s32[]{:T(128)}) %tuple.76), condition=%wide.region_8.9_spmd.clone, body=%wide.region_7.8_spmd.clone.sunk | while | flops 491523 | bytes 2359463 | solution.py:183
  57.6 3.4 collective-permute-start
  61.0 4.2 %collective-permute-done = bf16[12,64,128]{2,1,0:T(8,128)(2,1)S(1)} collective-permute-done((bf16[12,64,128]{2,1,0:T(8,128)(2,1)S(1)}, bf16[12,64,128]{2,1,0:T(8,128)(2,1)S(1)}, u32[]{:S(2)}, u32[]{:S(2)}) %collective-permute-start) | collective-permute-done | bytes 196640 | tf_op jit(solution)/shard_map/while/body/eval_jaxpr/ppermute | solution.py:17
  65.4 4.4 %collective-permute-start = (bf16[12,64,128]{2,1,0:T(8,128)(2,1)S(1)}, bf16[12,64,128]{2,1,0:T(8,128)(2,1)S(1)}, u32[]{:S(2)}, u32[]{:S(2)}) collective-permute-start(bf16[12,64,128]{2,1,0:T(8,128)(2,1)S(1)} %fusion.157), channel_id=1, source_target_pairs={{0,4},{4,8},{8,12},{12,16},{16,20},{20,24},{24,28},{1,5},{5,9},{9,... | collective-permute-start | bytes 589832 | tf_op jit(solution)/shard_map/while/body/eval_jaxpr/ppermute | solution.py:17
  69.8 3.4 collective-permute-done
  73.4 4.4 %collective-permute-start = (bf16[12,64,128]{2,1,0:T(8,128)(2,1)S(1)}, bf16[12,64,128]{2,1,0:T(8,128)(2,1)S(1)}, u32[]{:S(2)}, u32[]{:S(2)}) collective-permute-start(bf16[12,64,128]{2,1,0:T(8,128)(2,1)S(1)} %fusion.157), channel_id=1, source_target_pairs={{0,4},{4,8},{8,12},{12,16},{16,20},{20,24},{24,28},{1,5},{5,9},{9,... | collective-permute-start | bytes 589832 | tf_op jit(solution)/shard_map/while/body/eval_jaxpr/ppermute | solution.py:17
  77.8 3.2 collective-permute-done
  81.1 5.2 %collective-permute-start = (bf16[12,64,128]{2,1,0:T(8,128)(2,1)S(1)}, bf16[12,64,128]{2,1,0:T(8,128)(2,1)S(1)}, u32[]{:S(2)}, u32[]{:S(2)}) collective-permute-start(bf16[12,64,128]{2,1,0:T(8,128)(2,1)S(1)} %fusion.157), channel_id=1, source_target_pairs={{0,4},{4,8},{8,12},{12,16},{16,20},{20,24},{24,28},{1,5},{5,9},{9,... | collective-permute-start | bytes 589832 | tf_op jit(solution)/shard_map/while/body/eval_jaxpr/ppermute | solution.py:17
  86.3 3.2 collective-permute-done
  89.6 5.3 %collective-permute-start = (bf16[12,64,128]{2,1,0:T(8,128)(2,1)S(1)}, bf16[12,64,128]{2,1,0:T(8,128)(2,1)S(1)}, u32[]{:S(2)}, u32[]{:S(2)}) collective-permute-start(bf16[12,64,128]{2,1,0:T(8,128)(2,1)S(1)} %fusion.157), channel_id=1, source_target_pairs={{0,4},{4,8},{8,12},{12,16},{16,20},{20,24},{24,28},{1,5},{5,9},{9,... | collective-permute-start | bytes 589832 | tf_op jit(solution)/shard_map/while/body/eval_jaxpr/ppermute | solution.py:17
  95.0 3.2 collective-permute-done
  98.3 5.3 %collective-permute-start = (bf16[12,64,128]{2,1,0:T(8,128)(2,1)S(1)}, bf16[12,64,128]{2,1,0:T(8,128)(2,1)S(1)}, u32[]{:S(2)}, u32[]{:S(2)}) collective-permute-start(bf16[12,64,128]{2,1,0:T(8,128)(2,1)S(1)} %fusion.157), channel_id=1, source_target_pairs={{0,4},{4,8},{8,12},{12,16},{16,20},{20,24},{24,28},{1,5},{5,9},{9,... | collective-permute-start | bytes 589832 | tf_op jit(solution)/shard_map/while/body/eval_jaxpr/ppermute | solution.py:17
  103.6 3.7 collective-permute-done
  107.4 5.6 %collective-permute-start = (bf16[12,64,128]{2,1,0:T(8,128)(2,1)S(1)}, bf16[12,64,128]{2,1,0:T(8,128)(2,1)S(1)}, u32[]{:S(2)}, u32[]{:S(2)}) collective-permute-start(bf16[12,64,128]{2,1,0:T(8,128)(2,1)S(1)} %fusion.157), channel_id=1, source_target_pairs={{0,4},{4,8},{8,12},{12,16},{16,20},{20,24},{24,28},{1,5},{5,9},{9,... | collective-permute-start | bytes 589832 | tf_op jit(solution)/shard_map/while/body/eval_jaxpr/ppermute | solution.py:17
  113.0 3.2 collective-permute-done
  116.3 1.8 fusion.93
  118.2 16.8 %fusion.64 = f32[512,12,64]{0,2,1:T(8,128)} fusion(f32[512,12,64]{0,2,1:T(8,128)S(1)} %bitcast.158, f32[512,12,64]{0,2,1:T(8,128)S(1)} %fusion.93, f32[512,12,64]{0,2,1:T(8,128)} %fusion.90, f32[512,12]{0,1:T(8,128)S(1)} %bitcast.163, f32[512,512]{1,0:T(8,128)} %fusion.101, pred[512,512]{1,0:T(8,128)(4,1)S(1)} %copy-done.18, f32[12]{0:T(128)S(1)} %copy-done.35, ...), kind=kOutput, calls=%fused_computation.69 | convolution fusion | flops 2431254528 | bytes 7700528 | tf_op jit(solution)/shard_map/while/body/eval_jaxpr/tsh,shp->thp/dot_general | solution.py:117
  135.0 3.0 copy.68
  138.0 5.4 %multiply_reduce_fusion.1 = (f32[512]{0:T(512)S(1)}, f32[512,768]{1,0:T(8,128)}) fusion(f32[512,768]{1,0:T(8,128)} %copy.68, bf16[1536,768]{1,0:T(8,128)(2,1)} %param.30, bf16[512,1536]{1,0:T(8,128)(2,1)} %all-gather.3.cloned.1.call-done, f32[1536]{0:T(1024)S(1)} %copy-done.32, f32[512]{0:T(512)S(1)} %copy-done.28), kind=kOutput, calls=%fused_computation.71 | convolution fusion | flops 1214643712 | bytes 7088128 | tf_op jit(solution)/shard_map/dot_general | solution.py:74
  143.4 5.9 %psum.7 = f32[512]{0:T(512)S(1)} all-reduce(f32[512]{0:T(512)S(1)} %get-tuple-element.271), channel_id=1, replica_groups=mesh['seq'=8,'exp'=4] {'exp'}, use_global_device_ids=true, to_apply=%region_10.11 | all-reduce | flops 512 | bytes 4096 | tf_op jit(solution)/shard_map/psum | solution.py:204
  149.3 4.0 convolution_convert_fusion.1
  155.0 1.7 reduce-window.30
  157.4 3.4 scatter_custom_fusion
  160.9 23.7 %reduce-scatter.4.cloned.1.call-done = bf16[128,1536]{1,0:T(8,128)(2,1)} async-done(((bf16[512,1536]{1,0:T(8,128)(2,1)}), bf16[128,1536]{1,0:T(8,128)(2,1)}) %reduce-scatter.4.cloned.1.call-update) | async-done | bytes 393232 | tf_op jit(solution)/shard_map/reduce_scatter | solution.py:209
  184.6 1.2 multiply_reduce_fusion.2
  185.8 1.2 multiply_convert_fusion.3
  187.0 5.6 %gather_fusion = bf16[1024,1536]{1,0:T(8,128)(2,1)} fusion(bf16[129,1536]{1,0:T(8,128)(2,1)S(1)} %concatenate.19, s32[1024]{0:T(1024)S(1)} %fusion.117), kind=kCustom, calls=%fused_computation | custom fusion | bytes 6295552 | tf_op jit(solution)/shard_map/gather | solution.py:238
  192.6 5.7 %all-to-all-start = ((bf16[8,4,32,1536]{3,2,1,0:T(8,128)(2,1)}), bf16[8,4,32,1536]{3,2,1,0:T(8,128)(2,1)}, u32[]{:S(2)}, u32[]{:S(2)}) async-start(bf16[8,4,32,1536]{3,2,1,0:T(8,128)(2,1)} %bitcast.159), calls=%async_computation.2 | async-start | bytes 6291456 | tf_op jit(solution)/shard_map/all_to_all | solution.py:239
  199.2 1.7 broadcast_multiply_fusion
  201.0 2.1 broadcast.319.clone
  203.1 12.6 %while.31 = (s32[]{:T(128)}, f32[8,12,64,128]{3,2,1,0:T(8,128)}, s32[]{:T(128)}, pred[8]{0:T(512)(128)(4,1)S(1)}, s32[512]{0:T(512)S(1)}, /*index=5*/s32[8]{0:T(...) while((s32[]{:T(128)}, f32[8,12,64,128]{3,2,1,0:T(8,128)}, ...), condition=%wide.region_20.21_spmd, body=%wide.region_19.20_spmd.sunk | while | flops 604686848 | bytes 3534819 | solution.py:149
  209.3 1.1 constant_dynamic-slice_fusion.3
  210.9 2.8 fusion.156
  215.7 3.9 multiply_add_fusion
  219.9 4.1 %scatter_fusion = f32[8,12,64,128]{3,2,1,0:T(8,128)S(1)} fusion(f32[8,12,64,128]{3,2,1,0:T(8,128)S(1)} %broadcast.319, s32[8]{0:T(128)S(1)} %compare_select_fusion.6, f32[8,12,64,128]{3,2,1,0:T(8,128)} %multiply_add_fusion), kind=kCustom, calls=%fused_computation.4 | custom fusion | bytes 9437216 | tf_op jit(solution)/shard_map/scatter | solution.py:196
  224.1 1.5 convert_element_type.191
  225.6 54.8 %all-to-all-done = bf16[8,4,32,1536]{3,2,1,0:T(8,128)(2,1)} async-done(((bf16[8,4,32,1536]{3,2,1,0:T(8,128)(2,1)}), bf16[8,4,32,1536]{3,2,1,0:T(8,128)(2,1)}, u32[]{:S(2)}, u32[]{:S(2)}) %all-to-all-start) | async-done | bytes 3145760 | tf_op jit(solution)/shard_map/all_to_all | solution.py:239
  280.4 7.0 %fusion.33 = f32[4,8,32,512]{3,2,1,0:T(8,128)} fusion(bf16[4,1536,512]{2,1,0:T(8,128)(2,1)} %param.45, bf16[8,4,32,1536]{3,2,1,0:T(8,128)(2,1)} %all-to-all-done), kind=kOutput, calls=%fused_computation.34 | convolution fusion | flops 1610612736 | bytes 11534336 | tf_op jit(solution)/shard_map/secd,edf->secf/dot_general | solution.py:240
  287.4 9.7 %fusion.43 = bf16[8,4,32,1536]{3,2,0,1:T(8,128)(2,1)S(1)} fusion(bf16[4,512,1536]{2,1,0:T(8,128)(2,1)} %param.47, f32[4,8,32,512]{3,2,1,0:T(8,128)} %fusion.33, bf16[4,1536,512]{2,1,0:T(8,128)(2,1)} %param.46, bf16[8,4,32,1536]{3,2,1,0:T(8,128)(2,1)} %all-to-all-done), kind=kOutput, calls=%fused_computation.45 | convolution fusion | flops 3225944064 | bytes 20971520 | tf_op jit(solution)/shard_map/secf,efd->secd/dot_general | solution.py:243
  297.1 1.9 copy.76
  299.0 4.4 %all-to-all-start.1 = ((bf16[8,4,32,1536]{3,2,1,0:T(8,128)(2,1)}), bf16[8,4,32,1536]{3,2,1,0:T(8,128)(2,1)S(1)}, u32[]{:S(2)}, u32[]{:S(2)}) async-start(bf16[8,4,32,1536]{3,2,1,0:T(8,128)(2,1)} %copy.76), calls=%async_computation.3 | async-start | bytes 6291456 | tf_op jit(solution)/shard_map/all_to_all | solution.py:246
  303.4 3.0 fusion.136
  306.4 5.0 %convolution_convert_fusion = bf16[512,1536]{1,0:T(8,128)(2,1)} fusion(bf16[256,1536]{1,0:T(8,128)(2,1)} %param.44, bf16[512,1536]{1,0:T(8,128)(2,1)} %all-gather.5.cloned.1.call-done, bf16[1536,256]{1,0:T(8,128)(2,1)} %param.43, f32[512,256]{1,0:T(8,128)} %fusion.136), kind=kOutput, calls=%fused_computation.50 | convolution fusion | flops 806879232 | bytes 5242880 | tf_op jit(solution)/shard_map/dot_general | solution.py:220
  312.8 8.3 %reduce-scatter.8.cloned.1.call-done = bf16[1,12,64,128]{3,2,1,0:T(8,128)(2,1)} async-done(((bf16[8,12,64,128]{3,2,1,0:T(8,128)(2,1)}), bf16[1,12,64,128]{3,2,1,0:T(8,128)(2,1)}) %reduce-scatter.8.cloned.1.call-update) | async-done | bytes 196624 | tf_op jit(solution)/shard_map/reduce_scatter | solution.py:197
  321.1 1.7 convert_element_type.192
  322.8 56.0 %all-to-all-done.1 = bf16[8,4,32,1536]{3,2,1,0:T(8,128)(2,1)S(1)} async-done(((bf16[8,4,32,1536]{3,2,1,0:T(8,128)(2,1)}), bf16[8,4,32,1536]{3,2,1,0:T(8,128)(2,1)S(1)}, u32[]{:S(2)}, u32[]{:S(2)}) %all-to-all-start.1) | async-done | bytes 3145760 | tf_op jit(solution)/shard_map/all_to_all | solution.py:246
  378.8 3.9 gather_fusion.1
  382.7 5.0 %reshape.315 = f32[128,6,1536]{2,1,0:T(8,128)} reshape(bf16[768,1536]{1,0:T(8,128)(2,1)} %gather_fusion.1) | data formatting | bytes 7077888 | tf_op jit(solution)/shard_map/convert_element_type | solution.py:250
  387.7 6.2 %multiply_reduce_fusion = f32[128,1536]{1,0:T(8,128)} fusion(f32[128,6,1536]{2,1,0:T(8,128)} %reshape.315, f32[128,6]{1,0:T(8,128)S(1)} %copy-done.17), kind=kLoop, calls=%fused_computation.36 | loop fusion | flops 2162688 | bytes 5508096 | tf_op jit(solution)/shard_map/reduce_sum | solution.py:250
  393.9 2.1 add_convert_fusion
  (167 shorter events, 16.0 us)
Async XLA Ops:
  7.2 142.2 %copy-start = (bf16[768,1536]{1,0:T(8,128)(2,1)S(1)}, bf16[768,1536]{1,0:T(8,128)(2,1)}, u32[]{:S(2)}) copy-start(bf16[768,1536]{1,0:T(8,128)(2,1)} %param.40) | copy-start | bytes 7077892
  7.2 26.7 %copy-start.31 = (f32[1536]{0:T(1024)S(1)}, f32[1536]{0:T(1024)}, u32[]{:S(2)}) copy-start(f32[1536]{0:T(1024)} %param.29) | copy-start | bytes 18436
  7.2 24.8 %all-gather.3.cloned.1.call-start = ((), (), s32[]{:S(2)}) async-start(), calls=%async_computation.5 | async-start | bytes 1966080 | tf_op jit(solution)/shard_map/all_gather | solution.py:71
  7.9 176.7 %reduce-scatter.4.cloned.1.call-start = ((), (), s32[]{:S(2)}) async-start(), calls=%async_computation.6 | async-start | bytes 1966080 | tf_op jit(solution)/shard_map/reduce_scatter | solution.py:209
  32.0 1.9 copy-start.8
  33.9 7.7 %copy-start.27 = (f32[512]{0:T(512)}, f32[512]{0:T(512)S(1)}, u32[]{:S(2)}) copy-start(f32[512]{0:T(512)S(1)} %add_rsqrt_fusion.1) | copy-start | bytes 6148
  33.9 3.2 copy-start.29
  37.1 0.9 copy-start.9
  37.2 4.4 %copy-start.30 = (bf16[1536,12]{0,1:T(8,128)(2,1)S(1)}, bf16[1536,12]{0,1:T(8,128)(2,1)}, u32[]{:S(2)}) copy-start(bf16[1536,12]{0,1:T(8,128)(2,1)} %param.33) | copy-start | bytes 110596
  37.2 4.4 %copy-start.34 = (f32[12]{0:T(128)S(1)}, f32[12]{0:T(128)}, u32[]{:S(2)}) copy-start(f32[12]{0:T(128)} %param.36) | copy-start | bytes 148
  38.0 6.6 %collective-permute-start.1 = (bf16[3,1024]{1,0:T(4,128)(2,1)S(1)}, bf16[3,1024]{1,0:T(4,128)(2,1)S(1)}, u32[]{:S(2)}, u32[]{:S(2)}) collective-permute-start(bf16[3,1024]{1,0:T(4,128)(2,1)S(1)} %pad_maximum_fusion.2), channel_id=1, source_target_pairs={{0,4},{4,8},{8,12},{12,16},{16,20},{20,24},{24,28},{1,5},{5,9},{9,... | collective-permute-start | bytes 18440 | tf_op jit(solution)/shard_map/ppermute | solution.py:17
  43.8 0.9 copy-start.11
  44.6 10.5 %copy-start.14 = (f32[512,12]{0,1:T(8,128)}, f32[512,12]{0,1:T(8,128)S(1)}, u32[]{:S(2)}) copy-start(f32[512,12]{0,1:T(8,128)S(1)} %get-tuple-element.273) | copy-start | bytes 73732
  46.2 8.9 %copy-start.4 = (bf16[512,256]{1,0:T(8,128)(2,1)}, bf16[512,256]{1,0:T(8,128)(2,1)S(1)}, u32[]{:S(2)}) copy-start(bf16[512,256]{1,0:T(8,128)(2,1)S(1)} %multiply_convert_fusion.4) | copy-start | bytes 786436
  46.3 3.3 copy-start.10
  46.3 3.3 copy-start.23
  46.3 3.3 copy-start.24
  57.6 7.7 %collective-permute-start = (bf16[12,64,128]{2,1,0:T(8,128)(2,1)S(1)}, bf16[12,64,128]{2,1,0:T(8,128)(2,1)S(1)}, u32[]{:S(2)}, u32[]{:S(2)}) collective-permute-start(bf16[12,64,128]{2,1,0:T(8,128)(2,1)S(1)} %fusion.157), channel_id=1, source_target_pairs={{0,4},{4,8},{8,12},{12,16},{16,20},{20,24},{24,28},{1,5},{5,9},{9,... | collective-permute-start | bytes 589832 | tf_op jit(solution)/shard_map/while/body/eval_jaxpr/ppermute | solution.py:17
  65.4 7.8 %collective-permute-start = (bf16[12,64,128]{2,1,0:T(8,128)(2,1)S(1)}, bf16[12,64,128]{2,1,0:T(8,128)(2,1)S(1)}, u32[]{:S(2)}, u32[]{:S(2)}) collective-permute-start(bf16[12,64,128]{2,1,0:T(8,128)(2,1)S(1)} %fusion.157), channel_id=1, source_target_pairs={{0,4},{4,8},{8,12},{12,16},{16,20},{20,24},{24,28},{1,5},{5,9},{9,... | collective-permute-start | bytes 589832 | tf_op jit(solution)/shard_map/while/body/eval_jaxpr/ppermute | solution.py:17
  73.4 7.6 %collective-permute-start = (bf16[12,64,128]{2,1,0:T(8,128)(2,1)S(1)}, bf16[12,64,128]{2,1,0:T(8,128)(2,1)S(1)}, u32[]{:S(2)}, u32[]{:S(2)}) collective-permute-start(bf16[12,64,128]{2,1,0:T(8,128)(2,1)S(1)} %fusion.157), channel_id=1, source_target_pairs={{0,4},{4,8},{8,12},{12,16},{16,20},{20,24},{24,28},{1,5},{5,9},{9,... | collective-permute-start | bytes 589832 | tf_op jit(solution)/shard_map/while/body/eval_jaxpr/ppermute | solution.py:17
  81.1 8.4 %collective-permute-start = (bf16[12,64,128]{2,1,0:T(8,128)(2,1)S(1)}, bf16[12,64,128]{2,1,0:T(8,128)(2,1)S(1)}, u32[]{:S(2)}, u32[]{:S(2)}) collective-permute-start(bf16[12,64,128]{2,1,0:T(8,128)(2,1)S(1)} %fusion.157), channel_id=1, source_target_pairs={{0,4},{4,8},{8,12},{12,16},{16,20},{20,24},{24,28},{1,5},{5,9},{9,... | collective-permute-start | bytes 589832 | tf_op jit(solution)/shard_map/while/body/eval_jaxpr/ppermute | solution.py:17
  89.6 8.5 %collective-permute-start = (bf16[12,64,128]{2,1,0:T(8,128)(2,1)S(1)}, bf16[12,64,128]{2,1,0:T(8,128)(2,1)S(1)}, u32[]{:S(2)}, u32[]{:S(2)}) collective-permute-start(bf16[12,64,128]{2,1,0:T(8,128)(2,1)S(1)} %fusion.157), channel_id=1, source_target_pairs={{0,4},{4,8},{8,12},{12,16},{16,20},{20,24},{24,28},{1,5},{5,9},{9,... | collective-permute-start | bytes 589832 | tf_op jit(solution)/shard_map/while/body/eval_jaxpr/ppermute | solution.py:17
  98.3 9.0 %collective-permute-start = (bf16[12,64,128]{2,1,0:T(8,128)(2,1)S(1)}, bf16[12,64,128]{2,1,0:T(8,128)(2,1)S(1)}, u32[]{:S(2)}, u32[]{:S(2)}) collective-permute-start(bf16[12,64,128]{2,1,0:T(8,128)(2,1)S(1)} %fusion.157), channel_id=1, source_target_pairs={{0,4},{4,8},{8,12},{12,16},{16,20},{20,24},{24,28},{1,5},{5,9},{9,... | collective-permute-start | bytes 589832 | tf_op jit(solution)/shard_map/while/body/eval_jaxpr/ppermute | solution.py:17
  107.4 8.8 %collective-permute-start = (bf16[12,64,128]{2,1,0:T(8,128)(2,1)S(1)}, bf16[12,64,128]{2,1,0:T(8,128)(2,1)S(1)}, u32[]{:S(2)}, u32[]{:S(2)}) collective-permute-start(bf16[12,64,128]{2,1,0:T(8,128)(2,1)S(1)} %fusion.157), channel_id=1, source_target_pairs={{0,4},{4,8},{8,12},{12,16},{16,20},{20,24},{24,28},{1,5},{5,9},{9,... | collective-permute-start | bytes 589832 | tf_op jit(solution)/shard_map/while/body/eval_jaxpr/ppermute | solution.py:17
  116.2 1.9 copy-start.2
  116.3 1.9 copy-start.12
  116.3 1.9 copy-start.15
  116.3 1.9 copy-start.18
  116.3 1.9 copy-start.19
  116.3 1.9 copy-start.20
  116.3 1.9 copy-start.35
  135.0 3.0 copy-start.28
  135.0 3.0 copy-start.32
  138.0 11.3 %copy-start.33 = (f32[768]{0:T(1024)S(1)}, f32[768]{0:T(1024)}, u32[]{:S(2)}) copy-start(f32[768]{0:T(1024)} %param.39) | copy-start | bytes 9220
  153.3 0.7 copy-start.21
  153.3 7.5 %copy-start.26 = (s32[8]{0:T(128)S(1)}, s32[8]{0:T(128)}, u32[]{:S(2)}) copy-start(s32[8]{0:T(128)} %get-tuple-element.265) | copy-start | bytes 100
  153.3 31.3 %copy-start.3 = (bf16[128,1536]{1,0:T(8,128)(2,1)S(1)}, bf16[128,1536]{1,0:T(8,128)(2,1)}, u32[]{:S(2)}) copy-start(bf16[128,1536]{1,0:T(8,128)(2,1)} %param.28) | copy-start | bytes 1179652
  153.3 32.5 %copy-start.22 = (f32[1536]{0:T(1024)S(1)}, f32[1536]{0:T(1024)}, u32[]{:S(2)}) copy-start(f32[1536]{0:T(1024)} %param.41) | copy-start | bytes 18436
  187.0 5.6 %copy-start.7 = (bf16[128,1536]{1,0:T(8,128)(2,1)}, bf16[128,1536]{1,0:T(8,128)(2,1)S(1)}, u32[]{:S(2)}) copy-start(bf16[128,1536]{1,0:T(8,128)(2,1)S(1)} %multiply_convert_fusion.3) | copy-start | bytes 1179652
  192.6 5.8 %copy-start.36 = (s32[8]{0:T(128)S(1)}, s32[8]{0:T(128)}, u32[]{:S(2)}) copy-start(s32[8]{0:T(128)} %param.51) | copy-start | bytes 100
  192.6 5.8 %copy-start.13 = (f32[2,8,4,128]{3,1,2,0:T(8,128)S(1)}, f32[2,8,4,128]{3,1,2,0:T(8,128)}, u32[]{:S(2)}) copy-start(f32[2,8,4,128]{3,1,2,0:T(8,128)} %copy-done.11) | copy-start | bytes 98308
  192.6 6.6 %copy-start.5 = (bf16[512,256]{1,0:T(8,128)(2,1)S(1)}, bf16[512,256]{1,0:T(8,128)(2,1)}, u32[]{:S(2)}) copy-start(bf16[512,256]{1,0:T(8,128)(2,1)} %copy-done.4) | copy-start | bytes 786436
  192.6 6.6 %copy-start.16 = (f32[512,12]{0,1:T(8,128)S(1)}, f32[512,12]{0,1:T(8,128)}, u32[]{:S(2)}) copy-start(f32[512,12]{0,1:T(8,128)} %copy-done.14) | copy-start | bytes 73732
  192.6 87.8 %all-to-all-start = ((bf16[8,4,32,1536]{3,2,1,0:T(8,128)(2,1)}), bf16[8,4,32,1536]{3,2,1,0:T(8,128)(2,1)}, u32[]{:S(2)}, u32[]{:S(2)}) async-start(bf16[8,4,32,1536]{3,2,1,0:T(8,128)(2,1)} %bitcast.159), calls=%async_computation.2 | async-start | bytes 6291456 | tf_op jit(solution)/shard_map/all_to_all | solution.py:239
  198.3 105.1 %all-gather.5.cloned.1.call-start = ((), (), s32[]{:S(2)}) async-start(), calls=%async_computation.7 | async-start | bytes 1966080 | tf_op jit(solution)/shard_map/all_gather | solution.py:214
  200.9 120.2 %reduce-scatter.8.cloned.1.call-start = ((), (), s32[]{:S(2)}) async-start(), calls=%async_computation.9 | async-start | bytes 1769472 | tf_op jit(solution)/shard_map/reduce_scatter | solution.py:197
  299.0 79.8 %all-to-all-start.1 = ((bf16[8,4,32,1536]{3,2,1,0:T(8,128)(2,1)}), bf16[8,4,32,1536]{3,2,1,0:T(8,128)(2,1)S(1)}, u32[]{:S(2)}, u32[]{:S(2)}) async-start(bf16[8,4,32,1536]{3,2,1,0:T(8,128)(2,1)} %copy.76), calls=%async_computation.3 | async-start | bytes 6291456 | tf_op jit(solution)/shard_map/all_to_all | solution.py:246
  303.3 90.5 %reduce-scatter.6.cloned.1.call-start = ((), (), s32[]{:S(2)}) async-start(), calls=%async_computation.8 | async-start | bytes 1966080 | tf_op jit(solution)/shard_map/reduce_scatter | solution.py:219
  311.4 0.7 copy-start.25
  382.6 5.0 %copy-start.17 = (f32[128,6]{1,0:T(8,128)S(1)}, f32[128,6]{1,0:T(8,128)}, u32[]{:S(2)}) copy-start(f32[128,6]{1,0:T(8,128)} %copy.69) | copy-start | bytes 9220
  387.7 6.2 %copy-start.6 = (bf16[128,1536]{1,0:T(8,128)(2,1)S(1)}, bf16[128,1536]{1,0:T(8,128)(2,1)}, u32[]{:S(2)}) copy-start(bf16[128,1536]{1,0:T(8,128)(2,1)} %reduce-scatter.4.cloned.1.call-done) | copy-start | bytes 1179652
  387.7 8.3 %copy-start.1 = (bf16[768,1536]{1,0:T(8,128)(2,1)S(1)}, bf16[768,1536]{1,0:T(8,128)(2,1)}, u32[]{:S(2)}) copy-start(bf16[768,1536]{1,0:T(8,128)(2,1)} %param.40) | copy-start | bytes 7077892
Sparse Core Ops, SparseCore 0:
  9.6 22.3 all-gather.2
  153.5 31.0 reduce-scatter.3
  201.3 20.1 all-gather.4
  225.7 95.3 reduce-scatter.7
  323.5 52.5 reduce-scatter.5
where the time goes:
time: 407 us; the launch traced here: 403 us
  waiting for transfers between devices  180 us (44%)
  matrix products  65.5 us (16%)
  starting transfers between devices  47.4 us (12%)
  local copies, waits for them, and re-layouts  43.3 us (11%)
  other arithmetic  36.3 us (9%)
  between operations  17.5 us (4%)
  loops' own time  6.87 us (2%)
  blocking collectives  5.89 us (1%)
    all_to_all x1, waiting for transfers between devices, body(): lax.all_to_all(expert_out, 'seq', split_axis=0, concat_axis=0, tiled=True)  56 us
    all_to_all x1, waiting for transfers between devices, body(): lax.all_to_all(outgoing, 'seq', split_axis=0, concat_axis=0, tiled=True)  54.8 us
    ppermute x8, starting transfers between devices, from_behind(): return lax.ppermute(block, axis, route)  37.2 us
    ppermute x8, waiting for transfers between devices, from_behind(): return lax.ppermute(block, axis, route)  23.9 us
    reduce_scatter x1, waiting for transfers between devices, body(): lax.psum_scatter(mix_term.astype(jnp.bfloat16), 'exp', scatter_dimension=...  23.7 us
    dot_general x1, matrix products, block_step(): outputs = jnp.einsum('tsh,shp->thp', weights, drive, precision=highest)  16.8 us
    all_gather x1, waiting for transfers between devices, body(): stream = lax.all_gather(tokens, 'exp', axis=0, tiled=True)  12.4 us
    dot_general x1, matrix products, body(): jnp.einsum('secf,efd->secd', hidden, ex_down, preferred_element_type=jnp....  9.66 us
  transfers between devices with their start and end apart: 15, of which 12 were waited for; matrix products, arithmetic and copies ran while one was open for 21% of the time, Pallas kernels for 0%

commit v1 on v0

v1 whole, which is shorter than its diff:
```python
import functools
import jax
import jax.numpy as jnp
from jax import lax
from jax.experimental import pallas as pl
from jax.experimental.pallas import tpu as pltpu
from jax.sharding import PartitionSpec as P

DI = 3072


epsilon = 1e-05
highest = lax.Precision.HIGHEST


def from_behind(block, axis, distance):
    devices = range(lax.axis_size(axis))
    route = [(i - distance, i) for i in devices if i - distance in devices]
    return lax.ppermute(block, axis, route)


def rms_rows(values, gain):
    meansq = jnp.mean(values * values, axis=-1, keepdims=True)
    return values * lax.rsqrt(meansq + epsilon) * gain


LANES = 128
HALF = 64


def call(kernel, outs, scratch, flops, *operands):
    moved = sum(v.size * v.dtype.itemsize for v in operands)
    smem = [v.dtype == jnp.int32 and v.ndim == 1 for v in operands]
    return pl.pallas_call(
        kernel,
        out_shape=[jax.ShapeDtypeStruct(s, t) for s, t in outs],
        in_specs=[pl.BlockSpec(memory_space=pltpu.SMEM if m else pltpu.VMEM) for m in smem],
        out_specs=[pl.BlockSpec(memory_space=pltpu.VMEM) for _ in outs],
        scratch_shapes=scratch,
        compiler_params=pltpu.CompilerParams(vmem_limit_bytes=48 * 1024 * 1024),
        cost_estimate=pl.CostEstimate(flops=int(flops), bytes_accessed=moved, transcendentals=0),
    )(*operands)


def positions(shape, axis, start, lag=0):
    return lax.broadcasted_iota(jnp.int32, shape, axis) + (start - lag)


def segments(pos, meta, req_count):
    seg = jnp.zeros(pos.shape, jnp.int32)
    for req in range(req_count):
        seg = seg + (pos >= meta[1 + req]).astype(jnp.int32)
    return seg


def scalar_segment(pos, meta, req_count):
    seg = jnp.int32(0)
    for req in range(req_count):
        seg = seg + (pos >= meta[1 + req]).astype(jnp.int32)
    return seg


def before_segment(meta, req_count):
    start = meta[0]
    return jnp.where(start > 0, scalar_segment(start - 1, meta, req_count), -1)


def by_head(values, pair):
    rows = values.shape[0]
    lane = lax.broadcasted_iota(jnp.int32, (rows, LANES), 1)
    return jnp.where(lane < HALF, values[:, 2 * pair : 2 * pair + 1], values[:, 2 * pair + 1 : 2 * pair + 2])


def front_kernel(
    req_count, heads, meta, xin, bcin, dt_raw, edge, conv_x, conv_bc, dt_bias, a_log,
    xc, bc, drive, drive_wt, cum, cum_t, lead, packet, ext,
):
    rows, channels = xin.shape
    start = meta[0]
    ext[0:8, :] = edge[8:16, :].astype(jnp.float32)
    ext[8:, :channels] = xin[...].astype(jnp.float32)
    ext[8:, channels:] = bcin[...].astype(jnp.float32)
    shape = (rows, LANES)
    seg = segments(positions(shape, 0, start), meta, req_count)
    kept = []
    for lag in (3, 2, 1):
        pos = positions(shape, 0, start, lag)
        kept.append((segments(pos, meta, req_count) == seg) & (pos >= 0))
    kept.append(None)

    def conv(column, weight, offset):
        total = jnp.zeros(shape, jnp.float32)
        for tap in range(4):
            window = ext[5 + tap : 5 + tap + rows, column : column + LANES]
            term = weight[tap : tap + 1, offset : offset + LANES] * window
            total = total + (term if kept[tap] is None else jnp.where(kept[tap], term, 0.0))
        return (total * jax.nn.sigmoid(total)).astype(jnp.bfloat16)

    for part in range(2):
        bc[:, part * LANES : (part + 1) * LANES] = conv(channels + part * LANES, conv_bc, part * LANES)
    raw = dt_raw[...].astype(jnp.float32) + dt_bias[...]
    step = jnp.maximum(raw, 0.0) + jnp.log1p(jnp.exp(-jnp.abs(raw)))
    log_decay = -step * jnp.exp(a_log[...])
    lower = (
        lax.broadcasted_iota(jnp.int32, (rows, rows), 0)
        >= lax.broadcasted_iota(jnp.int32, (rows, rows), 1)
    ).astype(jnp.float32)
    total = jnp.dot(lower, log_decay, precision=highest, preferred_element_type=jnp.float32)
    cum[...] = total
    cum_t[...] = total.T
    seg_before = before_segment(meta, req_count)
    lead[...] = jnp.where(seg == seg_before, jnp.exp(total), 0.0)
    seg_end = total
    for req in range(req_count):
        row = jnp.clip(meta[1 + req] - 1 - start, 0, rows - 1)
        seg_end = jnp.where(seg == req, cum[pl.ds(row, 1), :], seg_end)
    weight = step * jnp.exp(jnp.minimum(seg_end - total, 0.0))
    seg_last = scalar_segment(start + rows - 1, meta, req_count)
    b_last = jnp.where(seg == seg_last, bc[:, :LANES].astype(jnp.float32), 0.0).astype(jnp.bfloat16)
    for pair in range(heads // 2):
        cols = slice(pair * LANES, (pair + 1) * LANES)
        values = conv(pair * LANES, conv_x, pair * LANES)
        xc[:, cols] = values
        wide = values.astype(jnp.float32)
        drive[:, cols] = (wide * by_head(step, pair)).astype(jnp.bfloat16)
        turned = (wide * by_head(weight, pair)).T.astype(jnp.bfloat16)
        drive_wt[cols, :] = turned
        packet[cols, :] = jnp.dot(turned, b_last, preferred_element_type=jnp.float32).astype(jnp.bfloat16)
    passing = jnp.where(seg_last == seg_before, jnp.exp(total[rows - 1 : rows, :]), 0.0)
    high = passing.astype(jnp.bfloat16).astype(jnp.float32)
    row = lax.broadcasted_iota(jnp.int32, (16, LANES), 0)
    packet[channels:, :] = jnp.where(row == 0, high, jnp.where(row == 1, passing - high, 0.0)).astype(jnp.bfloat16)


def local_kernel(req_count, heads, meta, bc, xc, drive, cum, cum_t, d_skip, mixed):
    rows = xc.shape[0]
    start = meta[0]
    tile = LANES
    lane = lax.broadcasted_iota(jnp.int32, (tile, LANES), 1)
    for i in range(rows // tile):
        at = slice(i * tile, (i + 1) * tile)
        width = (i + 1) * tile
        pos_t = positions((tile, width), 0, start + i * tile)
        pos_s = positions((tile, width), 1, start)
        seg_t = segments(positions((tile, LANES), 0, start + i * tile), meta, req_count)[:, 0:1]
        seg_s = segments(positions((8, width), 1, start), meta, req_count)[0:1, :]
        scores = lax.dot_general(
            bc[at, LANES:], bc[0:width, :LANES], (((1,), (1,)), ((), ())), preferred_element_type=jnp.float32
        )
        scores = jnp.where((seg_t == seg_s) & (pos_t >= pos_s), scores, 0.0)
        for pair in range(heads // 2):
            cols = slice(pair * LANES, (pair + 1) * LANES)
            parts = []
            for head in (2 * pair, 2 * pair + 1):
                gap = cum[at, head : head + 1] - cum_t[head : head + 1, 0:width]
                decayed = (scores * jnp.exp(jnp.minimum(gap, 0.0))).astype(jnp.bfloat16)
                parts.append(jnp.dot(decayed, drive[0:width, cols], preferred_element_type=jnp.float32))
            skip = by_head(d_skip[...], pair) * xc[at, cols].astype(jnp.float32)
            mixed[at, cols] = jnp.where(lane < HALF, parts[0], parts[1]) + skip


def cache_kernel(req_count, heads, meta, bc, drive_wt, cum, packets, state_in, placed):
    channels, rows = drive_wt.shape
    start = meta[0]
    hops = packets.shape[0]
    for head in range(heads):
        at = slice(head * HALF, (head + 1) * HALF)
        state = packets[hops - 1, at, :].astype(jnp.float32)
        for hop in range(hops - 2, -1, -1):
            passing = packets[hop, channels : channels + 16, head : head + 1].astype(jnp.float32)
            scale = passing[0:1] + passing[1:2]
            state = scale * state + packets[hop, at, :].astype(jnp.float32)
        state_in[at, :] = state.astype(jnp.bfloat16)
    seg = segments(positions((rows, LANES), 0, start), meta, req_count)
    seg_before = before_segment(meta, req_count)
    for req in range(req_count):
        slot = meta[1 + req_count + req]
        end = meta[1 + req] - 1 - start
        inside = (end >= 0) & (end < rows)

        @pl.when(inside)
        def _():
            b_own = jnp.where(seg == req, bc[:, :LANES].astype(jnp.float32), 0.0).astype(jnp.bfloat16)
            last = cum[pl.ds(jnp.clip(end, 0, rows - 1), 1), :]
            holding = jnp.where(seg_before == req, jnp.exp(last), 0.0)
            fresh = jnp.dot(drive_wt[...], b_own, preferred_element_type=jnp.float32)
            for head in range(heads):
                at = slice(head * HALF, (head + 1) * HALF)
                held = holding[:, head : head + 1] * state_in[at, :].astype(jnp.float32)
                placed[slot, at, :] = (fresh[at] + held).astype(jnp.bfloat16)

        @pl.when(jnp.logical_not(inside))
        def _():
            placed[slot] = jnp.zeros((channels, LANES), jnp.bfloat16)


def gate_kernel(heads, mixed, gate_raw, bc, state_in, lead, gain, gated, square):
    rows = mixed.shape[0]
    total = jnp.zeros((rows, LANES), jnp.float32)
    for pair in range(heads // 2):
        cols = slice(pair * LANES, (pair + 1) * LANES)
        carried = lax.dot_general(
            bc[:, LANES:], state_in[cols, :], (((1,), (1,)), ((), ())), preferred_element_type=jnp.float32
        )
        raw = gate_raw[:, cols].astype(jnp.float32)
        value = (mixed[:, cols] + by_head(lead[...], pair) * carried) * (raw * jax.nn.sigmoid(raw))
        total = total + value * value
        gated[:, cols] = (value * gain[:, cols]).astype(jnp.bfloat16)
    square[...] = jnp.broadcast_to(jnp.sum(total, axis=1, keepdims=True), (rows, LANES))


def body(
    tokens,
    in_gain,
    in_z,
    in_x,
    in_bc,
    in_dt,
    conv_x,
    conv_bc,
    dt_bias,
    a_log,
    d_skip,
    norm_gain,
    out_w,
    post_gain,
    sh_gate,
    sh_up,
    sh_down,
    ex_gate,
    ex_up,
    ex_down,
    routes,
    gates,
    lengths,
    cache_slot,
):
    seq_count = lax.axis_size("seq")
    own_rows = tokens.shape[0]
    width = tokens.shape[1]
    state_size = in_bc.shape[1] // 2
    local_heads = a_log.shape[0]
    head_width = conv_x.shape[1] // local_heads
    stream = lax.all_gather(tokens, "exp", axis=0, tiled=True)
    row_count = stream.shape[0]
    normed_in = rms_rows(stream.astype(jnp.float32), in_gain).astype(jnp.bfloat16)
    conv_in_x = jnp.dot(normed_in, in_x, preferred_element_type=jnp.float32).astype(jnp.bfloat16)
    conv_in_bc = jnp.dot(normed_in, in_bc, preferred_element_type=jnp.float32).astype(jnp.bfloat16)
    dt_raw = jnp.dot(normed_in, jnp.pad(in_dt, ((0, 0), (0, LANES - local_heads))), preferred_element_type=jnp.float32).astype(jnp.bfloat16)
    tail_rows = jnp.concatenate([conv_in_x[row_count - 16 :], conv_in_bc[row_count - 16 :]], axis=1)
    edge_rows = from_behind(tail_rows, "seq", 1)
    gate_raw = jnp.dot(normed_in, in_z, preferred_element_type=jnp.float32).astype(jnp.bfloat16)
    req_ends = jnp.cumsum(lengths)
    stream_start = lax.axis_index("seq") * row_count
    meta = jnp.concatenate([jnp.reshape(stream_start, (1,)), req_ends, cache_slot]).astype(jnp.int32)
    channels = conv_in_x.shape[1]

    def lanes(values):
        return jnp.pad(values, (0, LANES - values.shape[0]))[None]

    xc, bc, drive, drive_wt, cum, cum_t, lead, packet = call(
        functools.partial(front_kernel, lengths.shape[0], local_heads),
        [
            ((row_count, channels), jnp.bfloat16),
            ((row_count, 2 * state_size), jnp.bfloat16),
            ((row_count, channels), jnp.bfloat16),
            ((channels, row_count), jnp.bfloat16),
            ((row_count, LANES), jnp.float32),
            ((LANES, row_count), jnp.float32),
            ((row_count, LANES), jnp.float32),
            ((channels + 16, state_size), jnp.bfloat16),
        ],
        [pltpu.VMEM((row_count + 8, channels + 2 * state_size), jnp.float32)],
        3e8,
        meta,
        conv_in_x,
        conv_in_bc,
        dt_raw,
        edge_rows,
        conv_x,
        conv_bc,
        lanes(dt_bias),
        lanes(a_log),
    )
    longest = row_count * seq_count // 4
    hop_count = -(-longest // row_count)
    packets = [from_behind(packet, "seq", k + 1) for k in range(hop_count)]
    (mixed_local,) = call(
        functools.partial(local_kernel, lengths.shape[0], local_heads),
        [((row_count, channels), jnp.float32)],
        [],
        3e9,
        meta,
        bc,
        xc,
        drive,
        cum,
        cum_t,
        lanes(d_skip),
    )
    state_in, placed = call(
        functools.partial(cache_kernel, lengths.shape[0], local_heads),
        [
            ((channels, state_size), jnp.bfloat16),
            ((lengths.shape[0], channels, state_size), jnp.bfloat16),
        ],
        [],
        1e9,
        meta,
        bc,
        drive_wt,
        cum,
        jnp.stack(packets),
    )
    state_cache = (
        lax.psum_scatter(placed, "seq", scatter_dimension=0, tiled=True)
        .astype(jnp.float32)
        .reshape(1, local_heads, head_width, state_size)
    )
    gated, square_part = call(
        functools.partial(gate_kernel, local_heads),
        [((row_count, channels), jnp.bfloat16), ((row_count, LANES), jnp.float32)],
        [],
        1e9,
        mixed_local,
        gate_raw,
        bc,
        state_in,
        lead,
        norm_gain[None],
    )
    mix_term = jnp.dot(gated, out_w, preferred_element_type=jnp.float32)
    square_sum = lax.psum_scatter(square_part[:, 0], "exp", scatter_dimension=0, tiled=True)
    row_scale = lax.rsqrt(square_sum / DI + epsilon)[:, None]
    mixer_out = lax.psum_scatter(
        mix_term.astype(jnp.bfloat16), "exp", scatter_dimension=0, tiled=True
    ).astype(jnp.float32) * row_scale
    residual = tokens.astype(jnp.float32) + mixer_out
    normed = rms_rows(residual, post_gain).astype(jnp.bfloat16)
    normed_all = lax.all_gather(normed, "exp", axis=0, tiled=True)
    shared_hidden = (
        jax.nn.silu(jnp.dot(normed_all, sh_gate, preferred_element_type=jnp.float32))
        * jnp.dot(normed_all, sh_up, preferred_element_type=jnp.float32)
    ).astype(jnp.bfloat16)
    shared = lax.psum_scatter(
        jnp.dot(shared_hidden, sh_down, preferred_element_type=jnp.float32).astype(jnp.bfloat16),
        "exp",
        scatter_dimension=0,
        tiled=True,
    ).astype(jnp.float32)
    top_count = routes.shape[1]
    owned = ex_gate.shape[0]
    experts = owned * seq_count
    capacity = own_rows * top_count * 4 // (3 * experts)
    flat_routes = routes.reshape(-1)
    onehot = (flat_routes[:, None] == jnp.arange(experts, dtype=jnp.int32)[None, :]).astype(
        jnp.int32
    )
    slot_rank = jnp.sum(onehot * (jnp.cumsum(onehot, axis=0) - 1), axis=1)
    slot_idx = flat_routes * capacity + slot_rank
    owner_tok = jnp.arange(own_rows * top_count, dtype=jnp.int32) // top_count
    slot_tok = jnp.full((experts * capacity,), own_rows, jnp.int32).at[slot_idx].set(owner_tok)
    padded = jnp.concatenate([normed, jnp.zeros((1, width), jnp.bfloat16)])
    outgoing = padded[slot_tok].reshape(seq_count, owned, capacity, width)
    received = lax.all_to_all(outgoing, "seq", split_axis=0, concat_axis=0, tiled=True)
    gate_part = jnp.einsum("secd,edf->secf", received, ex_gate, preferred_element_type=jnp.float32)
    up_part = jnp.einsum("secd,edf->secf", received, ex_up, preferred_element_type=jnp.float32)
    hidden = (jax.nn.silu(gate_part) * up_part).astype(jnp.bfloat16)
    expert_out = jnp.einsum(
        "secf,efd->secd", hidden, ex_down, preferred_element_type=jnp.float32
    ).astype(jnp.bfloat16)
    returned = lax.all_to_all(expert_out, "seq", split_axis=0, concat_axis=0, tiled=True)
    picked = returned.reshape(experts * capacity, width)[slot_idx].reshape(
        own_rows, top_count, width
    )
    routed = jnp.sum(gates[:, :, None] * picked.astype(jnp.float32), axis=1)
    layer_out = (residual + shared + routed).astype(jnp.bfloat16)
    return (layer_out, state_cache)


def solution(mesh):
    placed = (
        P(("seq", "exp"), None),
        P(),
        P(None, "exp"),
        P(None, "exp"),
        P(),
        P(None, "exp"),
        P(None, "exp"),
        P(),
        P("exp"),
        P("exp"),
        P("exp"),
        P("exp"),
        P("exp", None),
        P(),
        P(None, "exp"),
        P(None, "exp"),
        P("exp", None),
        P("seq", None, None),
        P("seq", None, None),
        P("seq", None, None),
        P(("seq", "exp"), None),
        P(("seq", "exp"), None),
        P(),
        P(),
    )
    return jax.shard_map(
        body,
        mesh=mesh,
        in_specs=placed,
        out_specs=(P(("seq", "exp"), None), P("seq", "exp", None, None)),
        check_vma=False,
    )
```

time: 407 us -> 316 us (0.78)
  matrix products: 65.5 us -> 32.8 us
  starting transfers between devices: 47.4 us -> 20.2 us
  other arithmetic: 36.3 us -> 18.1 us
  local copies, waits for them, and re-layouts: 43.3 us -> 26.8 us
  Pallas kernels: 0 us -> 13.2 us
  loops' own time: 6.87 us -> 0 us
    dot_general x8 -> x2, matrix products: 31.6 us -> 3.17 us  [the longest x1 2.54 us: body(): mix_term = jnp.dot(gated, out_w, preferred_element_type=jnp.float32)]
    all_to_all x1, waiting for transfers between devices: 54.8 us -> 82.1 us  [body(): lax.all_to_all(outgoing, 'seq', split_axis=0, concat_axis=0, tiled=True)]
    ppermute x8 -> x3, starting transfers between devices: 37.2 us -> 10.6 us  [from_behind(): return lax.ppermute(block, axis, route)]
    ppermute x8 -> x3, waiting for transfers between devices: 23.9 us -> 0.36 us  [from_behind(): return lax.ppermute(block, axis, route)]
    pallas_call x0 -> x4, Pallas kernels: none -> 13.2 us  [call(): pl.pallas_call(kernel, out_shape=[jax.ShapeDtypeStruct(s, t) for s, t in...]
    convert_element_type x19 -> x0, other arithmetic: 8.36 us -> none  [the longest x1 2.53 us: block_step(): drive = drive_x.astype(jnp.float32) * step_rows[:, :, None]]
    reduce_scatter x1, waiting for transfers between devices: 8.28 us -> 0.01 us  [body(): lax.psum_scatter(placed, 'seq', scatter_dimension=0, tiled=True)]
    all_gather x1, waiting for transfers between devices: 12.4 us -> 20.4 us  [body(): stream = lax.all_gather(tokens, 'exp', axis=0, tiled=True)]
  transfers between devices with their start and end apart: 15 -> 10, of which waited for: 12 -> 5; matrix products, arithmetic and copies ran while one was open for 21% -> 19% of each run, Pallas kernels for 0% -> 1%
where the time goes in v1:
time: 316 us; the launch traced here: 314 us
  waiting for transfers between devices  182 us (58%)
  matrix products  32.8 us (10%)
  local copies, waits for them, and re-layouts  26.8 us (8%)
  starting transfers between devices  20.2 us (6%)
  other arithmetic  18.1 us (6%)
  between operations  14.8 us (5%)
  Pallas kernels  13.2 us (4%)
  blocking collectives  5.95 us (2%)
    all_to_all x1, waiting for transfers between devices, body(): lax.all_to_all(outgoing, 'seq', split_axis=0, concat_axis=0, tiled=True)  82.1 us
    all_to_all x1, waiting for transfers between devices, body(): lax.all_to_all(expert_out, 'seq', split_axis=0, concat_axis=0, tiled=True)  62.1 us
    all_gather x1, waiting for transfers between devices, body(): stream = lax.all_gather(tokens, 'exp', axis=0, tiled=True)  20.4 us
    reduce_scatter x1, waiting for transfers between devices, body(): lax.psum_scatter(mix_term.astype(jnp.bfloat16), 'exp', scatter_dimension=...  15.8 us
    pallas_call x4, Pallas kernels, call(): pl.pallas_call(kernel, out_shape=[jax.ShapeDtypeStruct(s, t) for s, t in...  13.2 us
    ppermute x3, starting transfers between devices, from_behind(): return lax.ppermute(block, axis, route)  10.6 us
    dot_general x1, matrix products, body(): jnp.einsum('secf,efd->secd', hidden, ex_down, preferred_element_type=jnp....  10.4 us
  transfers between devices with their start and end apart: 10, of which 5 were waited for; matrix products, arithmetic and copies ran while one was open for 19% of the time, Pallas kernels for 1%

profile of v1, /device:TPU:0, one launch (start us, length us, event | category | flops | bytes accessed | tf_op | source)
XLA Modules:
  0.0 314.4 jit_solution(9004616026953212261)
XLA Ops:
  7.2 0.0 all-gather.3.cloned.1.call-start
  7.2 0.7 all-gather.3.cloned.1.call-update
  7.9 0.0 reduce-scatter.4.cloned.1.call-start
  8.0 0.7 broadcast_in_dim.15.gain
  8.7 0.8 reduce-window.19
  9.5 0.7 pad_bitcast_fusion.d_skip
  10.1 0.7 pad_add_fusion.meta
  10.9 0.7 pad_bitcast_fusion.1
  11.6 20.4 %all-gather.3.cloned.1.call-done = bf16[512,1536]{1,0:T(8,128)(2,1)} async-done(((bf16[128,1536]{1,0:T(8,128)(2,1)}), bf16[512,1536]{1,0:T(8,128)(2,1)}) %all-gather.3.cloned.1.call-update) | async-done | bytes 1572880 | tf_op jit(solution)/shard_map/all_gather | solution.py:244
  32.0 1.8 fusion.12
  33.8 2.4 convolution_convert_fusion.4.bcin
  36.2 0.4 copy-done.12
  36.6 1.4 convolution_convert_fusion.3.xin
  38.1 3.4 %collective-permute-start = (bf16[16,1024]{1,0:T(8,128)(2,1)S(1)}, bf16[16,1024]{1,0:T(8,128)(2,1)S(1)}, u32[]{:S(2)}, u32[]{:S(2)}) collective-permute-start(bf16[16,1024]{1,0:T(8,128)(2,1)S(1)} %pad_maximum_fusion.1), channel_id=1, source_target_pairs={{0,4},{4,8},{8,12},{12,16},{16,20},{20,24},{24,28},{1,5},{5,9},{9,... | collective-permute-start | bytes 98312 | tf_op jit(solution)/shard_map/ppermute | solution.py:19
  41.5 1.4 convolution_convert_fusion.2.gate_raw
  43.0 0.6 convolution_convert_fusion.5.dt_raw
  43.6 0.0 copy-done.2
  43.7 5.6 %shard_map.239 = (bf16[512,768]{1,0:T(8,128)(2,1)S(1)}, bf16[512,256]{1,0:T(8,128)(2,1)S(1)}, bf16[512,768]{1,0:T(8,128)(2,1)S(1)}, bf16[768,512]{1,0:T(8,128)(2...) custom-call(s32[17]{0:T(128)S(1)} %pad_add_fusion.meta, ...), custom_call_target="tpu_custom_call" | custom-call | flops 300000000 | bytes 1229892 | tf_op jit(solution)/shard_map/pallas_call | solution.py:34
  49.3 4.6 %collective-permute-start.2 = (bf16[784,128]{1,0:T(8,128)(2,1)S(1)}, bf16[784,128]{1,0:T(8,128)(2,1)S(1)}, u32[]{:S(2)}, u32[]{:S(2)}) collective-permute-start(bf16[784,128]{1,0:T(8,128)(2,1)S(1)} %get-tuple-element.20), channel_id=1, source_target_pairs={{0,8},{4,12},{8,16},{12,20},{16,24},{20,28},{1,9},{5,13},{9,17},{1... | collective-permute-start | bytes 602120 | tf_op jit(solution)/shard_map/ppermute | solution.py:19
  53.9 2.7 collective-permute-start.1
  56.5 3.3 %shard_map.240.mixed = f32[512,768]{1,0:T(8,128)S(1)} custom-call(s32[17]{0:T(128)S(1)} %pad_add_fusion.meta, bf16[512,256]{1,0:T(8,128)(2,1)S(1)} %get-tuple-element.14.bc, bf16[512,768]{1,0:T(8,128)(2,1)S(1)} %get-tuple-element.15.xc, bf16[512,768]{1,0:T(8,128)(2,1)S(1)} %get-tuple-element.16.drive, f32[512,128]{1,0:T(8,128)S(1)} %get-tuple-element.17.cum, ...), custom_call_target="tpu_custom_call" | custom-call | flops 3000000000 | bytes 2359876 | tf_op jit(solution)/shard_map/pallas_call | solution.py:34
  59.8 0.4 collective-permute-done.1
  60.2 3.1 shard_map.241
  63.4 1.2 shard_map.242
  64.6 2.5 convolution_convert_fusion.1
  67.1 0.0 reduce-scatter.4.cloned.1.call-update
  67.2 0.1 copy.36
  67.3 0.1 eq.29
  67.4 0.1 eq.25
  67.6 0.1 copy.35
  67.7 0.1 mul.108
  67.8 1.7 reduce-window.20
  69.6 0.3 slice_reduce_fusion.1
  69.9 0.6 dynamic-slice
  71.1 0.1 fusion.38
  71.3 3.4 %scatter_custom_fusion = s32[1024]{0:T(1024)S(1)} fusion(s32[768]{0:T(1024)S(1)} %fusion.44, s32[768]{0:T(1024)S(1)} %add_select_fusion, s32[]{:T(128)} %constant.55.clone.1), kind=kCustom, calls=%fused_computation.69 | custom fusion | bytes 4100 | tf_op jit(solution)/shard_map/scatter | solution.py:362
  74.7 0.1 slice_reduce_fusion
  74.8 6.0 %all-reduce.5 = f32[512]{0:T(512)S(1)} all-reduce(f32[512]{0:T(512)S(1)} %slice_reduce_fusion), channel_id=3, replica_groups=mesh['seq'=8,'exp'=4] {'exp'}, use_global_device_ids=true, to_apply=%region_3.4.clone | all-reduce | flops 512 | bytes 4096
  80.8 0.1 fusion.48
  80.8 15.8 %reduce-scatter.4.cloned.1.call-done = bf16[128,1536]{1,0:T(8,128)(2,1)} async-done(((bf16[512,1536]{1,0:T(8,128)(2,1)}), bf16[128,1536]{1,0:T(8,128)(2,1)}) %reduce-scatter.4.cloned.1.call-update) | async-done | bytes 393232 | tf_op jit(solution)/shard_map/reduce_scatter | solution.py:335
  96.7 1.3 multiply_reduce_fusion.1
  98.0 1.3 multiply_convert_fusion
  99.3 5.6 %gather_fusion = bf16[1024,1536]{1,0:T(8,128)(2,1)} fusion(bf16[129,1536]{1,0:T(8,128)(2,1)S(1)} %concatenate.11, s32[1024]{0:T(1024)S(1)} %fusion.42), kind=kCustom, calls=%fused_computation | custom fusion | bytes 6295552 | tf_op jit(solution)/shard_map/gather | solution.py:364
  104.9 5.5 %all-to-all-start = ((bf16[8,4,32,1536]{3,2,1,0:T(8,128)(2,1)}), bf16[8,4,32,1536]{3,2,1,0:T(8,128)(2,1)S(1)}, u32[]{:S(2)}, u32[]{:S(2)}) async-start(bf16[8,4,32,1536]{3,2,1,0:T(8,128)(2,1)} %bitcast.90), calls=%async_computation.2 | async-start | bytes 6291456 | tf_op jit(solution)/shard_map/all_to_all | solution.py:365
  110.4 0.0 all-gather.5.cloned.1.call-start
  110.5 0.7 all-gather.5.cloned.1.call-update
  111.2 0.3 reduce-scatter.8.cloned.1.call-start
  111.4 0.3 reduce-scatter.8.cloned.1.call-update
  111.8 82.1 %all-to-all-done = bf16[8,4,32,1536]{3,2,1,0:T(8,128)(2,1)S(1)} async-done(((bf16[8,4,32,1536]{3,2,1,0:T(8,128)(2,1)}), bf16[8,4,32,1536]{3,2,1,0:T(8,128)(2,1)S(1)}, u32[]{:S(2)}, u32[]{:S(2)}) %all-to-all-start) | async-done | bytes 3145760 | tf_op jit(solution)/shard_map/all_to_all | solution.py:365
  193.9 6.0 %fusion.4 = f32[4,8,32,512]{3,2,1,0:T(8,128)} fusion(bf16[4,1536,512]{2,1,0:T(8,128)(2,1)} %param.41, bf16[8,4,32,1536]{3,2,1,0:T(8,128)(2,1)S(1)} %all-to-all-done), kind=kOutput, calls=%fused_computation.7 | convolution fusion | flops 1610612736 | bytes 11534336 | tf_op jit(solution)/shard_map/secd,edf->secf/dot_general | solution.py:366
  199.8 10.4 %fusion.9 = bf16[8,4,32,1536]{3,2,0,1:T(8,128)(2,1)} fusion(bf16[4,512,1536]{2,1,0:T(8,128)(2,1)} %param.43, f32[4,8,32,512]{3,2,1,0:T(8,128)} %fusion.4, bf16[4,1536,512]{2,1,0:T(8,128)(2,1)} %param.42, bf16[8,4,32,1536]{3,2,1,0:T(8,128)(2,1)S(1)} %all-to-all-done), kind=kOutput, calls=%fused_computation.13 | convolution fusion | flops 3225944064 | bytes 20971520 | tf_op jit(solution)/shard_map/secf,efd->secd/dot_general | solution.py:369
  210.3 4.0 %copy.41 = bf16[8,4,32,1536]{3,2,1,0:T(8,128)(2,1)} copy(bf16[8,4,32,1536]{3,2,0,1:T(8,128)(2,1)} %fusion.9) | data formatting | bytes 6291456 | tf_op jit(solution)/shard_map/convert_element_type | solution.py:371
  214.3 3.7 %all-to-all-start.1 = ((bf16[8,4,32,1536]{3,2,1,0:T(8,128)(2,1)}), bf16[8,4,32,1536]{3,2,1,0:T(8,128)(2,1)S(1)}, u32[]{:S(2)}, u32[]{:S(2)}) async-start(bf16[8,4,32,1536]{3,2,1,0:T(8,128)(2,1)} %copy.41), calls=%async_computation.3 | async-start | bytes 6291456 | tf_op jit(solution)/shard_map/all_to_all | solution.py:372
  217.9 0.0 reduce-scatter.6.cloned.1.call-start
  218.0 0.0 all-gather.5.cloned.1.call-done
  218.0 3.0 fusion.56
  221.0 5.0 %convolution_convert_fusion = bf16[512,1536]{1,0:T(8,128)(2,1)} fusion(bf16[256,1536]{1,0:T(8,128)(2,1)} %param.40, bf16[512,1536]{1,0:T(8,128)(2,1)} %all-gather.5.cloned.1.call-done, bf16[1536,256]{1,0:T(8,128)(2,1)} %param.39, f32[512,256]{1,0:T(8,128)} %fusion.56), kind=kOutput, calls=%fused_computation.17 | convolution fusion | flops 806879232 | bytes 5242880 | tf_op jit(solution)/shard_map/dot_general | solution.py:346
  226.0 0.7 copy.34
  226.8 1.7 convert.2
  228.5 62.1 %all-to-all-done.1 = bf16[8,4,32,1536]{3,2,1,0:T(8,128)(2,1)S(1)} async-done(((bf16[8,4,32,1536]{3,2,1,0:T(8,128)(2,1)}), bf16[8,4,32,1536]{3,2,1,0:T(8,128)(2,1)S(1)}, u32[]{:S(2)}, u32[]{:S(2)}) %all-to-all-start.1) | async-done | bytes 3145760 | tf_op jit(solution)/shard_map/all_to_all | solution.py:372
  290.6 3.9 %gather_fusion.1 = bf16[768,1536]{1,0:T(8,128)(2,1)} fusion(bf16[1024,1536]{1,0:T(8,128)(2,1)S(1)} %bitcast.89, s32[1024]{0:T(1024)S(1)} %pad_clamp_fusion), kind=kCustom, calls=%fused_computation.1 | custom fusion | bytes 4721664 | tf_op jit(solution)/shard_map/gather | solution.py:373
  294.4 5.0 %reshape.124 = f32[128,6,1536]{2,1,0:T(8,128)} reshape(bf16[768,1536]{1,0:T(8,128)(2,1)} %gather_fusion.1) | data formatting | bytes 7077888 | tf_op jit(solution)/shard_map/convert_element_type | solution.py:376
  299.4 6.2 %multiply_reduce_fusion = f32[128,1536]{1,0:T(8,128)} fusion(f32[128,6,1536]{2,1,0:T(8,128)} %reshape.124, f32[128,6]{1,0:T(8,128)S(1)} %copy-done.8), kind=kLoop, calls=%fused_computation.9 | loop fusion | flops 2162688 | bytes 5508096 | tf_op jit(solution)/shard_map/reduce_sum | solution.py:376
  305.6 2.3 add_convert_fusion
  (51 shorter events, 0.3 us)
Async XLA Ops:
  7.2 57.4 %copy-start = (bf16[768,1536]{1,0:T(8,128)(2,1)S(1)}, bf16[768,1536]{1,0:T(8,128)(2,1)}, u32[]{:S(2)}) copy-start(bf16[768,1536]{1,0:T(8,128)(2,1)} %param.36) | copy-start | bytes 7077892
  7.2 24.8 %all-gather.3.cloned.1.call-start = ((), (), s32[]{:S(2)}) async-start(), calls=%async_computation.5 | async-start | bytes 1966080 | tf_op jit(solution)/shard_map/all_gather | solution.py:244
  7.9 88.7 %reduce-scatter.4.cloned.1.call-start = ((), (), s32[]{:S(2)}) async-start(), calls=%async_computation.6 | async-start | bytes 1966080 | tf_op jit(solution)/shard_map/reduce_scatter | solution.py:335
  33.8 2.5 copy-start.7
  33.8 2.9 copy-start.12
  33.8 2.9 copy-start.15
  36.6 4.9 %copy-start.13 = (bf16[1536,768]{1,0:T(8,128)(2,1)S(1)}, bf16[1536,768]{1,0:T(8,128)(2,1)}, u32[]{:S(2)}) copy-start(bf16[1536,768]{1,0:T(8,128)(2,1)} %param.26) | copy-start | bytes 7077892
  38.1 4.8 %copy-start.14 = (bf16[1536,12]{0,1:T(8,128)(2,1)S(1)}, bf16[1536,12]{0,1:T(8,128)(2,1)}, u32[]{:S(2)}) copy-start(bf16[1536,12]{0,1:T(8,128)(2,1)} %param.29) | copy-start | bytes 110596
  38.1 5.5 %collective-permute-start = (bf16[16,1024]{1,0:T(8,128)(2,1)S(1)}, bf16[16,1024]{1,0:T(8,128)(2,1)S(1)}, u32[]{:S(2)}, u32[]{:S(2)}) collective-permute-start(bf16[16,1024]{1,0:T(8,128)(2,1)S(1)} %pad_maximum_fusion.1), channel_id=1, source_target_pairs={{0,4},{4,8},{8,12},{12,16},{16,20},{20,24},{24,28},{1,5},{5,9},{9,... | collective-permute-start | bytes 98312 | tf_op jit(solution)/shard_map/ppermute | solution.py:19
  43.0 0.7 copy-start.2
  43.0 0.7 copy-start.3
  49.3 10.5 %collective-permute-start.2 = (bf16[784,128]{1,0:T(8,128)(2,1)S(1)}, bf16[784,128]{1,0:T(8,128)(2,1)S(1)}, u32[]{:S(2)}, u32[]{:S(2)}) collective-permute-start(bf16[784,128]{1,0:T(8,128)(2,1)S(1)} %get-tuple-element.20), channel_id=1, source_target_pairs={{0,8},{4,12},{8,16},{12,20},{16,24},{20,28},{1,9},{5,13},{9,17},{1... | collective-permute-start | bytes 602120 | tf_op jit(solution)/shard_map/ppermute | solution.py:19
  53.9 6.3 %collective-permute-start.1 = (bf16[784,128]{1,0:T(8,128)(2,1)S(1)}, bf16[784,128]{1,0:T(8,128)(2,1)S(1)}, u32[]{:S(2)}, u32[]{:S(2)}) collective-permute-start(bf16[784,128]{1,0:T(8,128)(2,1)S(1)} %get-tuple-element.20), channel_id=1, source_target_pairs={{0,4},{4,8},{8,12},{12,16},{16,20},{20,24},{24,28},{1,5},{5,9},{9,... | collective-permute-start | bytes 602120 | tf_op jit(solution)/shard_map/ppermute | solution.py:19
  64.6 2.6 copy-start.9
  67.1 2.8 copy-start.16
  67.1 29.5 %copy-start.4 = (bf16[128,1536]{1,0:T(8,128)(2,1)S(1)}, bf16[128,1536]{1,0:T(8,128)(2,1)}, u32[]{:S(2)}) copy-start(bf16[128,1536]{1,0:T(8,128)(2,1)} %param.24) | copy-start | bytes 1179652
  67.1 30.9 %copy-start.10 = (f32[1536]{0:T(1024)S(1)}, f32[1536]{0:T(1024)}, u32[]{:S(2)}) copy-start(f32[1536]{0:T(1024)} %param.37) | copy-start | bytes 18436
  99.3 5.7 %copy-start.6 = (bf16[128,1536]{1,0:T(8,128)(2,1)}, bf16[128,1536]{1,0:T(8,128)(2,1)S(1)}, u32[]{:S(2)}) copy-start(bf16[128,1536]{1,0:T(8,128)(2,1)S(1)} %multiply_convert_fusion) | copy-start | bytes 1179652
  104.9 88.9 %all-to-all-start = ((bf16[8,4,32,1536]{3,2,1,0:T(8,128)(2,1)}), bf16[8,4,32,1536]{3,2,1,0:T(8,128)(2,1)S(1)}, u32[]{:S(2)}, u32[]{:S(2)}) async-start(bf16[8,4,32,1536]{3,2,1,0:T(8,128)(2,1)} %bitcast.90), calls=%async_computation.2 | async-start | bytes 6291456 | tf_op jit(solution)/shard_map/all_to_all | solution.py:365
  110.4 107.6 %all-gather.5.cloned.1.call-start = ((), (), s32[]{:S(2)}) async-start(), calls=%async_computation.7 | async-start | bytes 1966080 | tf_op jit(solution)/shard_map/all_gather | solution.py:340
  111.2 115.6 %reduce-scatter.8.cloned.1.call-start = ((), (), s32[]{:S(2)}) async-start(), calls=%async_computation.9 | async-start | bytes 1769472 | tf_op jit(solution)/shard_map/reduce_scatter | solution.py:316
  214.3 76.3 %all-to-all-start.1 = ((bf16[8,4,32,1536]{3,2,1,0:T(8,128)(2,1)}), bf16[8,4,32,1536]{3,2,1,0:T(8,128)(2,1)S(1)}, u32[]{:S(2)}, u32[]{:S(2)}) async-start(bf16[8,4,32,1536]{3,2,1,0:T(8,128)(2,1)} %copy.41), calls=%async_computation.3 | async-start | bytes 6291456 | tf_op jit(solution)/shard_map/all_to_all | solution.py:372
  217.9 87.7 %reduce-scatter.6.cloned.1.call-start = ((), (), s32[]{:S(2)}) async-start(), calls=%async_computation.8 | async-start | bytes 1966080 | tf_op jit(solution)/shard_map/reduce_scatter | solution.py:345
  221.0 5.0 %copy-start.11 = (f32[128,6]{0,1:T(8,128)S(1)}, f32[128,6]{0,1:T(8,128)}, u32[]{:S(2)}) copy-start(f32[128,6]{0,1:T(8,128)} %param.45) | copy-start | bytes 9220
  294.4 5.0 %copy-start.8 = (f32[128,6]{1,0:T(8,128)S(1)}, f32[128,6]{1,0:T(8,128)}, u32[]{:S(2)}) copy-start(f32[128,6]{1,0:T(8,128)} %copy.34) | copy-start | bytes 9220
  299.4 6.2 %copy-start.5 = (bf16[128,1536]{1,0:T(8,128)(2,1)S(1)}, bf16[128,1536]{1,0:T(8,128)(2,1)}, u32[]{:S(2)}) copy-start(bf16[128,1536]{1,0:T(8,128)(2,1)} %reduce-scatter.4.cloned.1.call-done) | copy-start | bytes 1179652
  299.4 8.4 %copy-start.1 = (bf16[768,1536]{1,0:T(8,128)(2,1)S(1)}, bf16[768,1536]{1,0:T(8,128)(2,1)}, u32[]{:S(2)}) copy-start(bf16[768,1536]{1,0:T(8,128)(2,1)} %param.36) | copy-start | bytes 7077892
Sparse Core Ops, SparseCore 0:
  9.6 22.3 all-gather.2
  67.3 29.3 reduce-scatter.3
  113.5 20.1 all-gather.4
  137.3 88.3 reduce-scatter.7
  228.1 44.1 reduce-scatter.5

commit v2 on v1

--- a/solution.py
+++ b/solution.py
@@ -194,7 +194,7 @@
             placed[slot] = jnp.zeros((channels, LANES), jnp.bfloat16)
 
 
-def gate_kernel(heads, mixed, gate_raw, bc, state_in, lead, gain, gated, square):
+def gate_kernel(heads, mixed, gate_raw, bc, state_in, lead, gain, out_w, term, gated):
     rows = mixed.shape[0]
     total = jnp.zeros((rows, LANES), jnp.float32)
     for pair in range(heads // 2):
@@ -206,7 +206,227 @@
         value = (mixed[:, cols] + by_head(lead[...], pair) * carried) * (raw * jax.nn.sigmoid(raw))
         total = total + value * value
         gated[:, cols] = (value * gain[:, cols]).astype(jnp.bfloat16)
-    square[...] = jnp.broadcast_to(jnp.sum(total, axis=1, keepdims=True), (rows, LANES))
+    width = out_w.shape[1]
+    for column in range(0, width, 512):
+        product = jnp.dot(gated[...], out_w[:, column : column + 512], preferred_element_type=jnp.float32)
+        term[:, column : column + 512] = product.astype(jnp.bfloat16)
+    square = jnp.sum(total, axis=1, keepdims=True)
+    term[:, width:] = jnp.broadcast_to(square, (rows, LANES)).astype(jnp.bfloat16)
+
+
+def route_kernel(count, capacity, first, routing, dispatch, combine):
+    slots = dispatch.shape[1]
+    rows = dispatch.shape[2]
+    top = routing.shape[1] // 2
+    slot = lax.broadcasted_iota(jnp.int32, (rows, slots), 1)
+    expert = (first[0] + slot // capacity).astype(jnp.float32)
+    place = (slot % capacity).astype(jnp.float32)
+    lower = (
+        lax.broadcasted_iota(jnp.int32, (rows, rows), 0) >= lax.broadcasted_iota(jnp.int32, (rows, rows), 1)
+    ).astype(jnp.bfloat16)
+    for source in range(count):
+        at = slice(source * rows, (source + 1) * rows)
+        named = jnp.zeros((rows, slots), jnp.float32)
+        weight = jnp.zeros((rows, slots), jnp.float32)
+        for k in range(top):
+            hit = routing[at, k : k + 1] == expert
+            named = jnp.where(hit, 1.0, named)
+            weight = jnp.where(hit, routing[at, top + k : top + k + 1], weight)
+        rank = jnp.dot(lower, named.astype(jnp.bfloat16), preferred_element_type=jnp.float32) - 1.0
+        chosen = jnp.where(rank == place, named, 0.0)
+        dispatch[source] = chosen.T.astype(jnp.bfloat16)
+        combine[source] = (chosen * weight).astype(jnp.bfloat16)
+
+
+def ring_seq(place, count):
+    half = place // (count // 2)
+    return 2 * place * (1 - half) + (2 * (count - 1 - place) + 1) * half
+
+
+def ring_place(count):
+    me = lax.axis_index("seq")
+    column = lax.rem(me, 2)
+    depth = me // 2
+    return depth * (1 - column) + (count - 1 - depth) * column
+
+
+def ring_enter(count):
+    place = ring_place(count)
+    right = ring_seq(lax.rem(place + 1, count), count)
+    left = ring_seq(lax.rem(place + count - 1, count), count)
+    exp = lax.axis_index("exp")
+    barrier = pltpu.get_barrier_semaphore()
+    for neighbour in (left, right):
+        pl.semaphore_signal(barrier, inc=1, device_id=(neighbour, exp), device_id_type=pl.DeviceIdType.MESH)
+    pl.semaphore_wait(barrier, 2)
+    return place, (right, exp), (left, exp)
+
+
+def remote(source, target, send, receive, device):
+    return pltpu.make_async_remote_copy(
+        src_ref=source,
+        dst_ref=target,
+        send_sem=send,
+        recv_sem=receive,
+        device_id=device,
+        device_id_type=pl.DeviceIdType.MESH,
+    )
+
+
+def ring_experts_kernel(
+    count, normed, dispatch, gate_hbm, up_hbm, down_hbm, result,
+    blocks, rows_in, gate_w, up_w, down_w, weight_sem, send_sem, recv_sem,
+):
+    loads = []
+    for i, (source, target) in enumerate(((gate_hbm, gate_w), (up_hbm, up_w), (down_hbm, down_w))):
+        loads.append(pltpu.make_async_copy(source, target, weight_sem.at[i]))
+        loads[-1].start()
+    place, right, left = ring_enter(count)
+    own_rows = normed.shape[0]
+    owned = gate_w.shape[0]
+    capacity = dispatch.shape[1] // owned
+    middle = count // 2
+
+    def deal(slot, block):
+        source = ring_seq(lax.rem(place + count - slot, count), count)
+        picked = jnp.dot(dispatch[source], block[...], preferred_element_type=jnp.float32).astype(jnp.bfloat16)
+        for expert in range(owned):
+            rows_in[expert, slot * capacity : (slot + 1) * capacity, :] = picked[
+                expert * capacity : (expert + 1) * capacity
+            ]
+
+    flying = []
+    for step in range(1, middle + 1):
+        from_left, from_right = step - 1, (count - step + 1) % count
+        pair = []
+        for way, (held, device) in enumerate(((from_left, right), (from_right, left))):
+            source = normed if step == 1 else blocks.at[held]
+            if step < middle:
+                target = blocks.at[step if way == 0 else count - step]
+            else:
+                part = pl.ds(way * (own_rows // 2), own_rows // 2)
+                source = source.at[part]
+                target = blocks.at[middle, part]
+            pair.append(remote(source, target, send_sem.at[way, step], recv_sem.at[way, step], device))
+            pair[-1].start()
+        if step == 1:
+            deal(0, normed)
+        else:
+            deal(step - 1, blocks.at[step - 1])
+            deal(count - step + 1, blocks.at[count - step + 1])
+        for copy in pair:
+            copy.wait_recv()
+        flying += pair
+    deal(middle, blocks.at[middle])
+    for copy in flying:
+        copy.wait_send()
+    for load in loads:
+        load.wait()
+
+    def expert_step(expert, carry):
+        rows = rows_in[expert]
+        gate = jnp.dot(rows, gate_w[expert], preferred_element_type=jnp.float32)
+        up = jnp.dot(rows, up_w[expert], preferred_element_type=jnp.float32)
+        hidden = (gate * jax.nn.sigmoid(gate) * up).astype(jnp.bfloat16)
+        for column in range(0, result.shape[2], 512):
+            out = jnp.dot(hidden, down_w[expert, :, column : column + 512], preferred_element_type=jnp.float32)
+            result[expert, :, column : column + 512] = out.astype(jnp.bfloat16)
+        return carry
+
+    lax.fori_loop(0, owned, expert_step, 0)
+
+
+def ring_experts(normed, dispatch, ex_gate, ex_up, ex_down):
+    count = dispatch.shape[0]
+    owned = ex_gate.shape[0]
+    rows = count * dispatch.shape[1] // owned
+    own_rows, width = normed.shape
+    vmem, far = pl.BlockSpec(memory_space=pltpu.VMEM), pl.BlockSpec(memory_space=pl.ANY)
+    return pl.pallas_call(
+        functools.partial(ring_experts_kernel, count),
+        out_shape=jax.ShapeDtypeStruct((owned, rows, width), jnp.bfloat16),
+        in_specs=[vmem, vmem, far, far, far],
+        out_specs=vmem,
+        scratch_shapes=[
+            pltpu.VMEM((count, own_rows, width), jnp.bfloat16),
+            pltpu.VMEM((owned, rows, width), jnp.bfloat16),
+            pltpu.VMEM(ex_gate.shape, jnp.bfloat16),
+            pltpu.VMEM(ex_up.shape, jnp.bfloat16),
+            pltpu.VMEM(ex_down.shape, jnp.bfloat16),
+            pltpu.SemaphoreType.DMA((3,)),
+            pltpu.SemaphoreType.DMA((2, count // 2 + 1)),
+            pltpu.SemaphoreType.DMA((2, count // 2 + 1)),
+        ],
+        compiler_params=pltpu.CompilerParams(
+            collective_id=1, has_side_effects=True, vmem_limit_bytes=48 * 1024 * 1024
+        ),
+        cost_estimate=pl.CostEstimate(flops=40_000_000_000, bytes_accessed=30_000_000, transcendentals=0),
+    )(normed, dispatch, ex_gate, ex_up, ex_down)
+
+
+def ring_sum_kernel(count, outs, combine, tied, total, stage, landed, send_sem, recv_sem):
+    place, right, left = ring_enter(count)
+    owned, rows, width = outs.shape
+    capacity = rows // count
+    own_rows = combine.shape[1]
+    half, piece_rows = width // 2, own_rows // 2
+
+    def partial(slot, way, piece):
+        source = ring_seq(lax.rem(place + count - slot, count), count)
+        columns = slice(way * half, (way + 1) * half)
+        held = jnp.concatenate(
+            [outs[e, slot * capacity : (slot + 1) * capacity, columns] for e in range(owned)], axis=0
+        )
+        weights = combine[source, piece * piece_rows : (piece + 1) * piece_rows, :]
+        return jnp.dot(weights, held, preferred_element_type=jnp.float32)
+
+    flying = {}
+    for step in range(count):
+        for piece in range(2):
+            at = slice(piece * piece_rows, (piece + 1) * piece_rows)
+            for way, device in enumerate((right, left)):
+                slot = (step + 1) % count if way == 0 else (count - 1 - step) % count
+                value = partial(slot, way, piece)
+                if step > 0:
+                    flying[way, step - 1, piece].wait_recv()
+                    value = value + landed[way, step - 1, at, :].astype(jnp.float32)
+                if step == count - 1:
+                    total[at, way * half : (way + 1) * half] = value
+                    continue
+                stage[way, step, at, :] = value.astype(jnp.bfloat16)
+                copy = remote(
+                    stage.at[way, step, pl.ds(piece * piece_rows, piece_rows)],
+                    landed.at[way, step, pl.ds(piece * piece_rows, piece_rows)],
+                    send_sem.at[way, step, piece],
+                    recv_sem.at[way, step, piece],
+                    device,
+                )
+                copy.start()
+                flying[way, step, piece] = copy
+    for copy in flying.values():
+        copy.wait_send()
+
+
+def ring_sum(outs, combine, tied):
+    count, own_rows, _ = combine.shape
+    width = outs.shape[2]
+    vmem, far = pl.BlockSpec(memory_space=pltpu.VMEM), pl.BlockSpec(memory_space=pl.ANY)
+    return pl.pallas_call(
+        functools.partial(ring_sum_kernel, count),
+        out_shape=jax.ShapeDtypeStruct((own_rows, width), jnp.float32),
+        in_specs=[vmem, vmem, far],
+        out_specs=vmem,
+        scratch_shapes=[
+            pltpu.VMEM((2, count - 1, own_rows, width // 2), jnp.bfloat16),
+            pltpu.VMEM((2, count - 1, own_rows, width // 2), jnp.bfloat16),
+            pltpu.SemaphoreType.DMA((2, count - 1, 2)),
+            pltpu.SemaphoreType.DMA((2, count - 1, 2)),
+        ],
+        compiler_params=pltpu.CompilerParams(
+            collective_id=2, has_side_effects=True, vmem_limit_bytes=48 * 1024 * 1024
+        ),
+        cost_estimate=pl.CostEstimate(flops=40_000_000_000, bytes_accessed=10_000_000, transcendentals=0),
+    )(outs, combine, tied)
 
 
 def body(
@@ -242,6 +462,22 @@
     local_heads = a_log.shape[0]
     head_width = conv_x.shape[1] // local_heads
     stream = lax.all_gather(tokens, "exp", axis=0, tiled=True)
+    owned = ex_gate.shape[0]
+    capacity = own_rows * routes.shape[1] * 4 // (3 * owned * seq_count)
+    packed = jnp.concatenate([routes.astype(jnp.float32), gates], axis=1)
+    routing = lax.all_gather(packed, "seq", axis=0, tiled=True)
+    first = jnp.reshape(lax.axis_index("seq") * owned, (1,)).astype(jnp.int32)
+    dispatch, combine = call(
+        functools.partial(route_kernel, seq_count, capacity),
+        [
+            ((seq_count, owned * capacity, own_rows), jnp.bfloat16),
+            ((seq_count, own_rows, owned * capacity), jnp.bfloat16),
+        ],
+        [],
+        1e8,
+        first,
+        routing,
+    )
     row_count = stream.shape[0]
     normed_in = rms_rows(stream.astype(jnp.float32), in_gain).astype(jnp.bfloat16)
     conv_in_x = jnp.dot(normed_in, in_x, preferred_element_type=jnp.float32).astype(jnp.bfloat16)
@@ -317,63 +553,33 @@
         .astype(jnp.float32)
         .reshape(1, local_heads, head_width, state_size)
     )
-    gated, square_part = call(
+    (mix_term,) = call(
         functools.partial(gate_kernel, local_heads),
-        [((row_count, channels), jnp.bfloat16), ((row_count, LANES), jnp.float32)],
-        [],
-        1e9,
+        [((row_count, width + LANES), jnp.bfloat16)],
+        [pltpu.VMEM((row_count, channels), jnp.bfloat16)],
+        3e9,
         mixed_local,
         gate_raw,
         bc,
         state_in,
         lead,
         norm_gain[None],
-    )
-    mix_term = jnp.dot(gated, out_w, preferred_element_type=jnp.float32)
-    square_sum = lax.psum_scatter(square_part[:, 0], "exp", scatter_dimension=0, tiled=True)
-    row_scale = lax.rsqrt(square_sum / DI + epsilon)[:, None]
-    mixer_out = lax.psum_scatter(
-        mix_term.astype(jnp.bfloat16), "exp", scatter_dimension=0, tiled=True
-    ).astype(jnp.float32) * row_scale
+        out_w,
+    )
+    mix_sum = lax.psum_scatter(mix_term, "exp", scatter_dimension=0, tiled=True).astype(jnp.float32)
+    row_scale = lax.rsqrt(mix_sum[:, width : width + 1] / DI + epsilon)
+    mixer_out = mix_sum[:, :width] * row_scale
     residual = tokens.astype(jnp.float32) + mixer_out
     normed = rms_rows(residual, post_gain).astype(jnp.bfloat16)
     normed_all = lax.all_gather(normed, "exp", axis=0, tiled=True)
+    expert_out = ring_experts(normed, dispatch, ex_gate, ex_up, ex_down)
     shared_hidden = (
         jax.nn.silu(jnp.dot(normed_all, sh_gate, preferred_element_type=jnp.float32))
         * jnp.dot(normed_all, sh_up, preferred_element_type=jnp.float32)
     ).astype(jnp.bfloat16)
-    shared = lax.psum_scatter(
-        jnp.dot(shared_hidden, sh_down, preferred_element_type=jnp.float32).astype(jnp.bfloat16),
-        "exp",
-        scatter_dimension=0,
-        tiled=True,
-    ).astype(jnp.float32)
-    top_count = routes.shape[1]
-    owned = ex_gate.shape[0]
-    experts = owned * seq_count
-    capacity = own_rows * top_count * 4 // (3 * experts)
-    flat_routes = routes.reshape(-1)
-    onehot = (flat_routes[:, None] == jnp.arange(experts, dtype=jnp.int32)[None, :]).astype(
-        jnp.int32
-    )
-    slot_rank = jnp.sum(onehot * (jnp.cumsum(onehot, axis=0) - 1), axis=1)
-    slot_idx = flat_routes * capacity + slot_rank
-    owner_tok = jnp.arange(own_rows * top_count, dtype=jnp.int32) // top_count
-    slot_tok = jnp.full((experts * capacity,), own_rows, jnp.int32).at[slot_idx].set(owner_tok)
-    padded = jnp.concatenate([normed, jnp.zeros((1, width), jnp.bfloat16)])
-    outgoing = padded[slot_tok].reshape(seq_count, owned, capacity, width)
-    received = lax.all_to_all(outgoing, "seq", split_axis=0, concat_axis=0, tiled=True)
-    gate_part = jnp.einsum("secd,edf->secf", received, ex_gate, preferred_element_type=jnp.float32)
-    up_part = jnp.einsum("secd,edf->secf", received, ex_up, preferred_element_type=jnp.float32)
-    hidden = (jax.nn.silu(gate_part) * up_part).astype(jnp.bfloat16)
-    expert_out = jnp.einsum(
-        "secf,efd->secd", hidden, ex_down, preferred_element_type=jnp.float32
-    ).astype(jnp.bfloat16)
-    returned = lax.all_to_all(expert_out, "seq", split_axis=0, concat_axis=0, tiled=True)
-    picked = returned.reshape(experts * capacity, width)[slot_idx].reshape(
-        own_rows, top_count, width
-    )
-    routed = jnp.sum(gates[:, :, None] * picked.astype(jnp.float32), axis=1)
+    shared_term = jnp.dot(shared_hidden, sh_down, preferred_element_type=jnp.float32).astype(jnp.bfloat16)
+    shared = lax.psum_scatter(shared_term, "exp", scatter_dimension=0, tiled=True).astype(jnp.float32)
+    routed = ring_sum(expert_out, combine, shared_term)
     layer_out = (residual + shared + routed).astype(jnp.bfloat16)
     return (layer_out, state_cache)
 

time: 316 us -> 265 us (0.84)
  waiting for transfers between devices: 182 us -> 74.2 us
  Pallas kernels: 13.2 us -> 93.4 us
  blocking collectives: 5.95 us -> 35.7 us
  matrix products: 32.8 us -> 15.1 us
  local copies, waits for them, and re-layouts: 26.8 us -> 11 us
  starting transfers between devices: 20.2 us -> 11.6 us
  other arithmetic: 18.1 us -> 9.92 us
    all_to_all x2 -> x0, waiting for transfers between devices: 144 us -> none  [the longest x1 82.1 us: body(): lax.all_to_all(outgoing, 'seq', split_axis=0, concat_axis=0, tiled=True)]
    pallas_call x0 -> x2, Pallas kernels: none -> 76.7 us  [the longest x1 41.6 us: ring_experts(): pl.pallas_call(functools.partial(ring_experts_kernel, count), out_shape=j...]
    all_gather x0 -> x1, blocking collectives: none -> 35.7 us  [body(): routing = lax.all_gather(packed, 'seq', axis=0, tiled=True)]
    dot_general x3 -> x0, matrix products: 18.9 us -> none  [the longest x1 10.4 us: body(): jnp.einsum('secf,efd->secd', hidden, ex_down, preferred_element_type=jnp....]
    reduce_scatter x1, waiting for transfers between devices: 0.01 us -> 18.6 us  [body(): lax.psum_scatter(placed, 'seq', scatter_dimension=0, tiled=True)]
    reduce_scatter x2, waiting for transfers between devices: 15.8 us -> 29 us  [the longest x1 28.9 us: body(): lax.psum_scatter(mix_term, 'exp', scatter_dimension=0, tiled=True)]
    gather x2 -> x0, local copies, waits for them, and re-layouts: 9.47 us -> none  [the longest x1 5.61 us: body(): outgoing = padded[slot_tok].reshape(seq_count, owned, capacity, width)]
    all_to_all x2 -> x0, starting transfers between devices: 9.17 us -> none  [the longest x1 5.52 us: body(): lax.all_to_all(outgoing, 'seq', split_axis=0, concat_axis=0, tiled=True)]
  transfers between devices with their start and end apart: 10 -> 8, of which waited for: 5 -> 6; matrix products, arithmetic and copies ran while one was open for 19% -> 3% of each run, Pallas kernels for 1% -> 33%
where the time goes in v2:
time: 265 us
  Pallas kernels  93.4 us (35%)
  waiting for transfers between devices  74.2 us (28%)
  blocking collectives  35.7 us (13%)
  matrix products  15.1 us (6%)
  between operations  14.3 us (5%)
  starting transfers between devices  11.6 us (4%)
  local copies, waits for them, and re-layouts  11 us (4%)
  other arithmetic  9.92 us (4%)
    pallas_call x1, Pallas kernels, ring_experts(): pl.pallas_call(functools.partial(ring_experts_kernel, count), out_shape=j...  41.6 us
    all_gather x1, blocking collectives, body(): routing = lax.all_gather(packed, 'seq', axis=0, tiled=True)  35.7 us
    pallas_call x1, Pallas kernels, ring_sum(): pl.pallas_call(functools.partial(ring_sum_kernel, count), out_shape=jax.S...  35.1 us
    reduce_scatter x1, waiting for transfers between devices, body(): lax.psum_scatter(mix_term, 'exp', scatter_dimension=0, tiled=True)  28.9 us
    all_gather x1, waiting for transfers between devices, body(): stream = lax.all_gather(tokens, 'exp', axis=0, tiled=True)  21.8 us
    reduce_scatter x1, waiting for transfers between devices, body(): lax.psum_scatter(placed, 'seq', scatter_dimension=0, tiled=True)  18.6 us
    pallas_call x5, Pallas kernels, call(): pl.pallas_call(kernel, out_shape=[jax.ShapeDtypeStruct(s, t) for s, t in...  16.7 us
    ppermute x3, starting transfers between devices, from_behind(): return lax.ppermute(block, axis, route)  11 us
  transfers between devices with their start and end apart: 8, of which 6 were waited for; matrix products, arithmetic and copies ran while one was open for 3% of the time, Pallas kernels for 33%

profile of v2, /device:TPU:0, one launch (start us, length us, event | category | flops | bytes accessed | tf_op | source)
XLA Modules:
  0.0 265.3 jit_solution(9551621696731797704)
XLA Ops:
  7.2 0.0 copy-start
  7.2 0.0 all-gather.3.cloned.1.call-start
  7.2 0.7 all-gather.3.cloned.1.call-update
  7.9 0.0 reduce-scatter.8.cloned.1.call-start
  8.0 0.8 reduce-window.9
  8.8 0.7 pad_add_fusion.meta
  9.5 0.7 pad_bitcast_fusion.1
  10.2 21.8 %all-gather.3.cloned.1.call-done = bf16[512,1536]{1,0:T(8,128)(2,1)} async-done(((bf16[128,1536]{1,0:T(8,128)(2,1)}), bf16[512,1536]{1,0:T(8,128)(2,1)}) %all-gather.3.cloned.1.call-update) | async-done | bytes 1572880 | tf_op jit(solution)/shard_map/all_gather | solution.py:464
  32.0 1.8 fusion
  33.8 0.0 copy-start.27
  33.8 2.4 convolution_convert_fusion.3.bcin
  36.2 0.0 copy-start.26
  36.2 1.5 convolution_convert_fusion.2.xin
  37.7 0.0 copy-start.6
  37.7 3.4 %collective-permute-start = (bf16[16,1024]{1,0:T(8,128)(2,1)S(1)}, bf16[16,1024]{1,0:T(8,128)(2,1)S(1)}, u32[]{:S(2)}, u32[]{:S(2)}) collective-permute-start(bf16[16,1024]{1,0:T(8,128)(2,1)S(1)} %pad_maximum_fusion.1), channel_id=1, source_target_pairs={{0,4},{4,8},{8,12},{12,16},{16,20},{20,24},{24,28},{1,5},{5,9},{9,... | collective-permute-start | bytes 98312 | tf_op jit(solution)/shard_map/ppermute | solution.py:19
  41.1 0.6 convolution_convert_fusion.4.dt_raw
  41.7 0.9 collective-permute-done.edge
  42.7 5.6 %shard_map.239 = (bf16[512,768]{1,0:T(8,128)(2,1)S(1)}, bf16[512,256]{1,0:T(8,128)(2,1)S(1)}, bf16[512,768]{1,0:T(8,128)(2,1)S(1)}, bf16[768,512]{1,0:T(8,128)(2...) custom-call(s32[17]{0:T(128)S(1)} %pad_add_fusion.meta, ...), custom_call_target="tpu_custom_call" | custom-call | flops 300000000 | bytes 1229892 | tf_op jit(solution)/shard_map/pallas_call | solution.py:34
  48.3 0.0 copy-start.13
  48.3 0.7 copy-done.13
  49.0 5.1 %collective-permute-start.2 = (bf16[784,128]{1,0:T(8,128)(2,1)S(1)}, bf16[784,128]{1,0:T(8,128)(2,1)S(1)}, u32[]{:S(2)}, u32[]{:S(2)}) collective-permute-start(bf16[784,128]{1,0:T(8,128)(2,1)S(1)} %get-tuple-element.20), channel_id=1, source_target_pairs={{0,8},{4,12},{8,16},{12,20},{16,24},{20,28},{1,9},{5,13},{9,17},{1... | collective-permute-start | bytes 602120 | tf_op jit(solution)/shard_map/ppermute | solution.py:19
  54.2 2.5 collective-permute-start.1
  56.7 1.0 collective-permute-done.2
  57.7 2.2 collective-permute-done.1
  59.9 0.0 copy-start.23
  59.9 0.0 copy-start.28
  60.0 1.3 shard_map.241
  61.3 1.1 copy-done.2
  62.4 0.7 copy-done.15
  63.1 0.0 reduce-scatter.8.cloned.1.call-update
  63.1 0.2 reduce-scatter.4.cloned.1.call-start
  63.4 0.0 copy-start.12
  63.4 3.7 %convolution_convert_fusion.1.gate_raw = bf16[512,768]{1,0:T(8,128)(2,1)S(1)} fusion(bf16[1536,768]{1,0:T(8,128)(2,1)} %param.26, bf16[512,1536]{1,0:T(8,128)(2,1)} %all-gather.3.cloned.1.call-done, f32[1536]{0:T(1024)S(1)} %copy-done.27, f32[512]{0:T(512)S(1)} %add_rsqrt_fusion), kind=kOutput, calls=%fused_computation.6 | convolution fusion | flops 1211498496 | bytes 4726784 | tf_op jit(solution)/shard_map/dot_general | solution.py:488
  67.1 3.4 %shard_map.240.mixed = f32[512,768]{1,0:T(8,128)S(1)} custom-call(s32[17]{0:T(128)S(1)} %pad_add_fusion.meta, bf16[512,256]{1,0:T(8,128)(2,1)S(1)} %get-tuple-element.14.bc, bf16[512,768]{1,0:T(8,128)(2,1)S(1)} %get-tuple-element.15.xc, bf16[512,768]{1,0:T(8,128)(2,1)S(1)} %copy-done.8, f32[512,128]{1,0:T(8,128)S(1)} %copy-done.12, ...), custom_call_target="tpu_custom_call" | custom-call | flops 3000000000 | bytes 2359876 | tf_op jit(solution)/shard_map/pallas_call | solution.py:34
  70.5 0.0 copy-start.25
  70.6 4.1 %shard_map.242 = bf16[512,1664]{1,0:T(8,128)(2,1)S(1)} custom-call(f32[512,768]{1,0:T(8,128)S(1)} %shard_map.240.mixed, bf16[512,768]{1,0:T(8,128)(2,1)S(1)} %convolution_convert_fusion.1.gate_raw, bf16[512,256]{1,0:T(8,128)(2,1)S(1)} %get-tuple-element.14.bc, bf16[768,128]{1,0:T(8,128)(2,1)S(1)} %copy-done.16, f32[512,128]{1,0:T(8,128)S(1)} %copy-done.10, ...), custom_call_target="tpu_custom_call" | custom-call | flops 3000000000 | bytes 5442560 | tf_op jit(solution)/shard_map/pallas_call | solution.py:34
  74.7 1.2 copy-done.1
  76.0 0.0 reduce-scatter.4.cloned.1.call-update
  76.0 0.0 copy-start.22
  76.0 0.0 all-gather.5.cloned.1.call-start
  76.1 0.1 copy.30
  76.2 35.7 %all_gather.11.routing = f32[1024,12]{1,0:T(8,128)S(1)} all-gather(f32[128,12]{1,0:T(8,128)S(1)} %copy.30), channel_id=1, replica_groups=mesh['seq'=8,'exp'=4] {'seq'}, dimensions={0}, use_global_device_ids=true | all-gather | bytes 55296 | tf_op jit(solution)/shard_map/all_gather | solution.py:468
  111.9 2.3 shard_map.243
  114.2 18.6 %reduce-scatter.8.cloned.1.call-done = bf16[1,768,128]{2,1,0:T(8,128)(2,1)} async-done(((bf16[8,768,128]{2,1,0:T(8,128)(2,1)}), bf16[1,768,128]{2,1,0:T(8,128)(2,1)}) %reduce-scatter.8.cloned.1.call-update) | async-done | bytes 196624 | tf_op jit(solution)/shard_map/reduce_scatter | solution.py:552
  132.8 1.7 convert.1
  134.5 28.9 %reduce-scatter.4.cloned.1.call-done = bf16[128,1664]{1,0:T(8,128)(2,1)} async-done(((bf16[512,1664]{1,0:T(8,128)(2,1)}), bf16[128,1664]{1,0:T(8,128)(2,1)}) %reduce-scatter.4.cloned.1.call-update) | async-done | bytes 426000 | tf_op jit(solution)/shard_map/reduce_scatter | solution.py:569
  163.4 1.1 convert_element_type.56
  164.5 0.1 fusion.14
  164.6 0.3 multiply_reduce_fusion
  164.9 0.5 copy-done.19
  165.4 1.0 multiply_convert_fusion.normed
  166.4 0.0 all-gather.5.cloned.1.call-update
  166.5 0.3 reduce-scatter.6.cloned.1.call-start
  166.7 1.0 copy-done.4
  167.7 41.6 %shard_map.244.outs = bf16[4,256,1536]{2,1,0:T(8,128)(2,1)S(1)} custom-call(bf16[128,1536]{1,0:T(8,128)(2,1)S(1)} %copy-done.4, bf16[8,128,128]{2,1,0:T(8,128)(2,1)S(1)} %get-tuple-element.23.dispatch, bf16[4,1536,512]{2,1,0:T(8,128)(2,1)} %gate_hbm.1, bf16[4,1536,512]{2,1,0:T(8,128)(2,1)} %up_hbm.1, bf16[4,512,1536]{2,1,0:T(8,128)(2,1)} %down_hbm.1), custom_call_target="tpu_custom_call" | custom-call | flops 40000000000 | bytes 30000000 | tf_op jit(solution)/shard_map/pallas_call | solution.py:345
  209.4 1.6 copy-done.17
  211.0 2.2 fusion.21
  213.2 4.8 %convolution_convert_fusion.tied = bf16[512,1536]{1,0:T(8,128)(2,1)} fusion(bf16[256,1536]{1,0:T(8,128)(2,1)} %param.40, bf16[512,1536]{1,0:T(8,128)(2,1)} %all-gather.5.cloned.1.call-done, bf16[1536,256]{1,0:T(8,128)(2,1)} %param.39, f32[512,256]{1,0:T(8,128)S(1)} %fusion.21), kind=kOutput, calls=%fused_computation.5 | convolution fusion | flops 806879232 | bytes 5242880 | tf_op jit(solution)/shard_map/dot_general | solution.py:580
  218.0 0.0 reduce-scatter.6.cloned.1.call-update
  218.0 1.4 copy-done.3
  219.4 1.9 copy-done.18
  221.3 35.1 %shard_map.245 = f32[128,1536]{1,0:T(8,128)S(1)} custom-call(bf16[4,256,1536]{2,1,0:T(8,128)(2,1)S(1)} %copy-done.18, bf16[8,128,128]{2,1,0:T(8,128)(2,1)S(1)} %get-tuple-element.24.combine, bf16[512,1536]{1,0:T(8,128)(2,1)S(1)} %copy-done.3), custom_call_target="tpu_custom_call" | custom-call | flops 40000000000 | bytes 10000000 | tf_op jit(solution)/shard_map/pallas_call | solution.py:414
  256.4 0.0 reduce-scatter.6.cloned.1.call-done
  256.4 2.3 add_convert_fusion
  (50 shorter events, 0.2 us)
Async XLA Ops:
  7.2 29.0 %copy-start = (bf16[1536,768]{1,0:T(8,128)(2,1)S(1)}, bf16[1536,768]{1,0:T(8,128)(2,1)}, u32[]{:S(2)}) copy-start(bf16[1536,768]{1,0:T(8,128)(2,1)} %param.27) | copy-start | bytes 7077892
  7.2 24.8 %all-gather.3.cloned.1.call-start = ((), (), s32[]{:S(2)}) async-start(), calls=%async_computation.3 | async-start | bytes 1966080 | tf_op jit(solution)/shard_map/all_gather | solution.py:464
  7.9 124.9 %reduce-scatter.8.cloned.1.call-start = ((), (), s32[]{:S(2)}) async-start(), calls=%async_computation.7 | async-start | bytes 1769472 | tf_op jit(solution)/shard_map/reduce_scatter | solution.py:552
  33.8 2.4 copy-start.21
  33.8 2.4 copy-start.27
  36.2 4.9 %copy-start.26 = (bf16[1536,12]{0,1:T(8,128)(2,1)S(1)}, bf16[1536,12]{0,1:T(8,128)(2,1)}, u32[]{:S(2)}) copy-start(bf16[1536,12]{0,1:T(8,128)(2,1)} %param.29) | copy-start | bytes 110596
  37.7 5.0 %copy-start.5 = (f32[4,768]{1,0:T(4,128)S(1)}, f32[4,768]{1,0:T(4,128)}, u32[]{:S(2)}) copy-start(f32[4,768]{1,0:T(4,128)} %conv_x.1) | copy-start | bytes 36868
  37.7 5.0 %copy-start.6 = (f32[4,256]{1,0:T(4,128)S(1)}, f32[4,256]{1,0:T(4,128)}, u32[]{:S(2)}) copy-start(f32[4,256]{1,0:T(4,128)} %conv_bc.1) | copy-start | bytes 12292
  37.7 5.0 %collective-permute-start = (bf16[16,1024]{1,0:T(8,128)(2,1)S(1)}, bf16[16,1024]{1,0:T(8,128)(2,1)S(1)}, u32[]{:S(2)}, u32[]{:S(2)}) collective-permute-start(bf16[16,1024]{1,0:T(8,128)(2,1)S(1)} %pad_maximum_fusion.1), channel_id=1, source_target_pairs={{0,4},{4,8},{8,12},{12,16},{16,20},{20,24},{24,28},{1,5},{5,9},{9,... | collective-permute-start | bytes 98312 | tf_op jit(solution)/shard_map/ppermute | solution.py:19
  48.3 0.7 copy-start.13
  49.0 10.9 %copy-start.7 = (bf16[512,768]{1,0:T(8,128)(2,1)}, bf16[512,768]{1,0:T(8,128)(2,1)S(1)}, u32[]{:S(2)}) copy-start(bf16[512,768]{1,0:T(8,128)(2,1)S(1)} %get-tuple-element.16.drive) | copy-start | bytes 2359300
  49.0 12.2 %copy-start.9 = (f32[512,128]{1,0:T(8,128)}, f32[512,128]{1,0:T(8,128)S(1)}, u32[]{:S(2)}) copy-start(f32[512,128]{1,0:T(8,128)S(1)} %get-tuple-element.22.lead) | copy-start | bytes 786436
  49.0 12.2 %copy-start.11 = (f32[512,128]{1,0:T(8,128)}, f32[512,128]{1,0:T(8,128)S(1)}, u32[]{:S(2)}) copy-start(f32[512,128]{1,0:T(8,128)S(1)} %get-tuple-element.17.cum) | copy-start | bytes 786436
  49.0 8.6 %collective-permute-start.2 = (bf16[784,128]{1,0:T(8,128)(2,1)S(1)}, bf16[784,128]{1,0:T(8,128)(2,1)S(1)}, u32[]{:S(2)}, u32[]{:S(2)}) collective-permute-start(bf16[784,128]{1,0:T(8,128)(2,1)S(1)} %get-tuple-element.20), channel_id=1, source_target_pairs={{0,8},{4,12},{8,16},{12,20},{16,24},{20,28},{1,9},{5,13},{9,17},{1... | collective-permute-start | bytes 602120 | tf_op jit(solution)/shard_map/ppermute | solution.py:19
  54.2 5.7 %collective-permute-start.1 = (bf16[784,128]{1,0:T(8,128)(2,1)S(1)}, bf16[784,128]{1,0:T(8,128)(2,1)S(1)}, u32[]{:S(2)}, u32[]{:S(2)}) collective-permute-start(bf16[784,128]{1,0:T(8,128)(2,1)S(1)} %get-tuple-element.20), channel_id=1, source_target_pairs={{0,4},{4,8},{8,12},{12,16},{16,20},{20,24},{24,28},{1,5},{5,9},{9,... | collective-permute-start | bytes 602120 | tf_op jit(solution)/shard_map/ppermute | solution.py:19
  59.9 3.4 %copy-start.23 = (f32[768]{0:T(1024)S(1)}, f32[768]{0:T(1024)}, u32[]{:S(2)}) copy-start(f32[768]{0:T(1024)} %param.35) | copy-start | bytes 9220
  59.9 3.4 %copy-start.28 = (f32[12]{0:T(128)S(1)}, f32[12]{0:T(128)}, u32[]{:S(2)}) copy-start(f32[12]{0:T(128)} %param.34) | copy-start | bytes 148
  61.2 1.2 copy-start.2
  62.4 0.7 copy-start.15
  63.1 100.3 %reduce-scatter.4.cloned.1.call-start = ((), (), s32[]{:S(2)}) async-start(), calls=%async_computation.4 | async-start | bytes 2129920 | tf_op jit(solution)/shard_map/reduce_scatter | solution.py:569
  63.4 3.7 %copy-start.8 = (bf16[512,768]{1,0:T(8,128)(2,1)S(1)}, bf16[512,768]{1,0:T(8,128)(2,1)}, u32[]{:S(2)}) copy-start(bf16[512,768]{1,0:T(8,128)(2,1)} %copy-done.7) | copy-start | bytes 2359300
  63.4 3.7 %copy-start.12 = (f32[512,128]{1,0:T(8,128)S(1)}, f32[512,128]{1,0:T(8,128)}, u32[]{:S(2)}) copy-start(f32[512,128]{1,0:T(8,128)} %copy-done.11) | copy-start | bytes 786436
  63.4 3.7 %copy-start.14 = (f32[128,512]{1,0:T(8,128)S(1)}, f32[128,512]{1,0:T(8,128)}, u32[]{:S(2)}) copy-start(f32[128,512]{1,0:T(8,128)} %copy-done.13) | copy-start | bytes 786436
  67.1 3.4 %copy-start.10 = (f32[512,128]{1,0:T(8,128)S(1)}, f32[512,128]{1,0:T(8,128)}, u32[]{:S(2)}) copy-start(f32[512,128]{1,0:T(8,128)} %copy-done.9) | copy-start | bytes 786436
  67.1 3.4 %copy-start.16 = (bf16[768,128]{1,0:T(8,128)(2,1)S(1)}, bf16[768,128]{1,0:T(8,128)(2,1)}, u32[]{:S(2)}) copy-start(bf16[768,128]{1,0:T(8,128)(2,1)} %copy-done.15) | copy-start | bytes 589828
  70.5 5.5 %copy-start.24 = (s32[128,6]{0,1:T(8,128)S(1)}, s32[128,6]{0,1:T(8,128)}, u32[]{:S(2)}) copy-start(s32[128,6]{0,1:T(8,128)} %param.44) | copy-start | bytes 9220
  70.5 5.5 %copy-start.25 = (f32[128,6]{0,1:T(8,128)S(1)}, f32[128,6]{0,1:T(8,128)}, u32[]{:S(2)}) copy-start(f32[128,6]{0,1:T(8,128)} %param.45) | copy-start | bytes 9220
  74.7 1.2 copy-start.1
  76.0 88.7 %copy-start.20 = (bf16[128,1536]{1,0:T(8,128)(2,1)S(1)}, bf16[128,1536]{1,0:T(8,128)(2,1)}, u32[]{:S(2)}) copy-start(bf16[128,1536]{1,0:T(8,128)(2,1)} %param.24) | copy-start | bytes 1179652
  76.0 89.4 %copy-start.22 = (f32[1536]{0:T(1024)S(1)}, f32[1536]{0:T(1024)}, u32[]{:S(2)}) copy-start(f32[1536]{0:T(1024)} %param.37) | copy-start | bytes 18436
  76.0 135.0 %all-gather.5.cloned.1.call-start = ((), (), s32[]{:S(2)}) async-start(), calls=%async_computation.5 | async-start | bytes 1966080 | tf_op jit(solution)/shard_map/all_gather | solution.py:574
  164.5 0.9 copy-start.19
  166.5 89.9 %reduce-scatter.6.cloned.1.call-start = ((), (), s32[]{:S(2)}) async-start(), calls=%async_computation.6 | async-start | bytes 1966080 | tf_op jit(solution)/shard_map/reduce_scatter | solution.py:581
  166.7 1.0 copy-start.4
  209.4 1.6 copy-start.17
  218.0 1.4 copy-start.3
  219.4 1.9 copy-start.18
Sparse Core Ops, SparseCore 0:
  9.6 22.3 all-gather.2
  63.2 69.5 reduce-scatter.7
  135.5 27.8 reduce-scatter.3
  166.6 19.6 all-gather.4
  218.1 26.4 reduce-scatter.5

commit v3 on v2

--- a/solution.py
+++ b/solution.py
@@ -214,28 +214,156 @@
     term[:, width:] = jnp.broadcast_to(square, (rows, LANES)).astype(jnp.bfloat16)
 
 
-def route_kernel(count, capacity, first, routing, dispatch, combine):
-    slots = dispatch.shape[1]
-    rows = dispatch.shape[2]
-    top = routing.shape[1] // 2
-    slot = lax.broadcasted_iota(jnp.int32, (rows, slots), 1)
-    expert = (first[0] + slot // capacity).astype(jnp.float32)
-    place = (slot % capacity).astype(jnp.float32)
-    lower = (
-        lax.broadcasted_iota(jnp.int32, (rows, rows), 0) >= lax.broadcasted_iota(jnp.int32, (rows, rows), 1)
-    ).astype(jnp.bfloat16)
-    for source in range(count):
-        at = slice(source * rows, (source + 1) * rows)
-        named = jnp.zeros((rows, slots), jnp.float32)
-        weight = jnp.zeros((rows, slots), jnp.float32)
-        for k in range(top):
-            hit = routing[at, k : k + 1] == expert
-            named = jnp.where(hit, 1.0, named)
-            weight = jnp.where(hit, routing[at, top + k : top + k + 1], weight)
-        rank = jnp.dot(lower, named.astype(jnp.bfloat16), preferred_element_type=jnp.float32) - 1.0
-        chosen = jnp.where(rank == place, named, 0.0)
-        dispatch[source] = chosen.T.astype(jnp.bfloat16)
-        combine[source] = (chosen * weight).astype(jnp.bfloat16)
+def exp_partners():
+    seq, me = lax.axis_index("seq"), lax.axis_index("exp")
+    core = lax.rem(me, 2)
+    row = me // 2
+    across = (seq, (1 - row) * 2 + core)
+    beside = (seq, row * 2 + 1 - core)
+    barrier = pltpu.get_barrier_semaphore()
+    for device in (across, beside):
+        pl.semaphore_signal(barrier, inc=1, device_id=device, device_id_type=pl.DeviceIdType.MESH)
+    pl.semaphore_wait(barrier, 2)
+    return row, core, across, beside
+
+
+def gather_kernel(tokens, gain, normed, landed, send_sem, recv_sem):
+    row, core, across, beside = exp_partners()
+    rows = tokens.shape[0]
+    pieces = [pl.ds(p * (rows // 2), rows // 2) for p in range(2)]
+
+    def put(block, at, part):
+        values = block.astype(jnp.float32)
+        base = pl.multiple_of((at * 2 + part) * (rows // 2), rows // 2)
+        normed[pl.ds(base, rows // 2), :] = rms_rows(values, gain[...]).astype(jnp.bfloat16)
+
+    over, side, onward = [], [], []
+    for p, piece in enumerate(pieces):
+        over.append(remote(tokens.at[piece], landed.at[0, piece], send_sem.at[0, p], recv_sem.at[0, p], across))
+        over[-1].start()
+    for p, piece in enumerate(pieces):
+        side.append(remote(tokens.at[piece], landed.at[1, piece], send_sem.at[1, p], recv_sem.at[1, p], beside))
+        side[-1].start()
+    for p, piece in enumerate(pieces):
+        put(tokens[piece, :], row * 2 + core, p)
+    for p, piece in enumerate(pieces):
+        side[p].wait_recv()
+        put(landed[1, piece, :], row * 2 + 1 - core, p)
+    for p, piece in enumerate(pieces):
+        over[p].wait_recv()
+        onward.append(
+            remote(landed.at[0, piece], landed.at[2, piece], send_sem.at[2, p], recv_sem.at[2, p], beside)
+        )
+        onward[-1].start()
+        put(landed[0, piece, :], (1 - row) * 2 + core, p)
+    for p, piece in enumerate(pieces):
+        onward[p].wait_recv()
+        put(landed[2, piece, :], (1 - row) * 2 + 1 - core, p)
+    for copy in over + side + onward:
+        copy.wait_send()
+
+
+def remote_params(number):
+    return pltpu.CompilerParams(collective_id=number, has_side_effects=True, vmem_limit_bytes=48 * 1024 * 1024)
+
+
+def gather_normed(tokens, gain):
+    rows, width = tokens.shape
+    count = lax.axis_size("exp")
+    if count != 4:
+        stream = lax.all_gather(tokens, "exp", axis=0, tiled=True)
+        return rms_rows(stream.astype(jnp.float32), gain).astype(jnp.bfloat16)
+    vmem = pl.BlockSpec(memory_space=pltpu.VMEM)
+    return pl.pallas_call(
+        gather_kernel,
+        out_shape=jax.ShapeDtypeStruct((count * rows, width), jnp.bfloat16),
+        in_specs=[vmem, vmem],
+        out_specs=vmem,
+        scratch_shapes=[
+            pltpu.VMEM((3, rows, width), jnp.bfloat16),
+            pltpu.SemaphoreType.DMA((3, 2)),
+            pltpu.SemaphoreType.DMA((3, 2)),
+        ],
+        compiler_params=remote_params(3),
+    )(tokens, gain[None])
+
+
+def finish_rows(total, tokens, gain):
+    width = tokens.shape[1]
+    scale = lax.rsqrt(total[:, width : width + 1] / DI + epsilon)
+    residual = tokens.astype(jnp.float32) + total[:, :width] * scale
+    return residual, rms_rows(residual, gain).astype(jnp.bfloat16)
+
+
+def sum_kernel(term, tokens, gain, packed, residual, block, beside_in, across_in, stage, send_sem, recv_sem):
+    row, core, across, beside = exp_partners()
+    rows, width = tokens.shape
+    part_rows = rows // 2
+
+    def part_of(owner_row, owner_core, part):
+        base = ((owner_row * 2 + owner_core) * 2 + part) * part_rows
+        return pl.ds(pl.multiple_of(base, part_rows), part_rows)
+
+    side, over = {}, []
+    for far in range(2):
+        owner_row = 1 - row if far == 0 else row
+        for part in range(2):
+            at = pl.ds(part * part_rows, part_rows)
+            copy = remote(
+                term.at[part_of(owner_row, 1 - core, part)],
+                beside_in.at[far, at],
+                send_sem.at[far, part],
+                recv_sem.at[far, part],
+                beside,
+            )
+            copy.start()
+            side[far, part] = copy
+    for part in range(2):
+        at = pl.ds(part * part_rows, part_rows)
+        side[0, part].wait_recv()
+        pair = term[part_of(1 - row, core, part), :].astype(jnp.float32) + beside_in[0, at, :].astype(jnp.float32)
+        stage[at, :] = pair.astype(jnp.bfloat16)
+        over.append(remote(stage.at[at], across_in.at[at], send_sem.at[2, part], recv_sem.at[2, part], across))
+        over[-1].start()
+    block[:, width:] = packed[...]
+    for part in range(2):
+        at = pl.ds(part * part_rows, part_rows)
+        side[1, part].wait_recv()
+        total = term[part_of(row, core, part), :].astype(jnp.float32) + beside_in[1, at, :].astype(jnp.float32)
+        over[part].wait_recv()
+        total = total + across_in[at, :].astype(jnp.float32)
+        kept, normed = finish_rows(total, tokens[at, :], gain[...])
+        residual[at, :] = kept
+        block[at, :width] = normed
+    for copy in list(side.values()) + over:
+        copy.wait_send()
+
+
+def sum_rows(term, tokens, gain, packed):
+    rows, width = tokens.shape
+    wide = term.shape[1]
+    if lax.axis_size("exp") != 4:
+        total = lax.psum_scatter(term, "exp", scatter_dimension=0, tiled=True).astype(jnp.float32)
+        residual, normed = finish_rows(total, tokens, gain)
+        return residual, jnp.concatenate([normed, packed], axis=1)
+    vmem = pl.BlockSpec(memory_space=pltpu.VMEM)
+    return pl.pallas_call(
+        sum_kernel,
+        out_shape=[
+            jax.ShapeDtypeStruct((rows, width), jnp.float32),
+            jax.ShapeDtypeStruct((rows, wide), jnp.bfloat16),
+        ],
+        in_specs=[vmem] * 4,
+        out_specs=[vmem] * 2,
+        scratch_shapes=[
+            pltpu.VMEM((2, rows, wide), jnp.bfloat16),
+            pltpu.VMEM((rows, wide), jnp.bfloat16),
+            pltpu.VMEM((rows, wide), jnp.bfloat16),
+            pltpu.SemaphoreType.DMA((3, 2)),
+            pltpu.SemaphoreType.DMA((3, 2)),
+        ],
+        compiler_params=remote_params(4),
+    )(term, tokens, gain[None], packed)
 
 
 def ring_seq(place, count):
@@ -274,7 +402,7 @@
 
 
 def ring_experts_kernel(
-    count, normed, dispatch, gate_hbm, up_hbm, down_hbm, result,
+    count, top, capacity, normed, gate_hbm, up_hbm, down_hbm, result, combine,
     blocks, rows_in, gate_w, up_w, down_w, weight_sem, send_sem, recv_sem,
 ):
     loads = []
@@ -284,12 +412,31 @@
     place, right, left = ring_enter(count)
     own_rows = normed.shape[0]
     owned = gate_w.shape[0]
-    capacity = dispatch.shape[1] // owned
+    width = result.shape[2]
     middle = count // 2
+    shape = (own_rows, owned * capacity)
+    lane = lax.broadcasted_iota(jnp.int32, shape, 1)
+    expert_id = (lax.axis_index("seq") * owned + lane // capacity).astype(jnp.float32)
+    rank_id = (lane % capacity).astype(jnp.float32)
+    lower = (
+        lax.broadcasted_iota(jnp.int32, (own_rows, own_rows), 0)
+        >= lax.broadcasted_iota(jnp.int32, (own_rows, own_rows), 1)
+    )
+    lower = jnp.where(lower, 1.0, 0.0).astype(jnp.bfloat16)
 
     def deal(slot, block):
-        source = ring_seq(lax.rem(place + count - slot, count), count)
-        picked = jnp.dot(dispatch[source], block[...], preferred_element_type=jnp.float32).astype(jnp.bfloat16)
+        routing = block[:, width:].astype(jnp.float32)
+        named = jnp.zeros(shape, jnp.float32)
+        weight = jnp.zeros(shape, jnp.float32)
+        for k in range(top):
+            hit = routing[:, k : k + 1] == expert_id
+            named = jnp.where(hit, 1.0, named)
+            weight = jnp.where(hit, routing[:, top + k : top + k + 1], weight)
+        rank = jnp.dot(lower, named.astype(jnp.bfloat16), preferred_element_type=jnp.float32) - 1.0
+        chosen = jnp.where(rank == rank_id, named, 0.0)
+        combine[slot] = (chosen * weight).astype(jnp.bfloat16)
+        dispatch = chosen.T.astype(jnp.bfloat16)
+        picked = jnp.dot(dispatch, block[:, :width], preferred_element_type=jnp.float32).astype(jnp.bfloat16)
         for expert in range(owned):
             rows_in[expert, slot * capacity : (slot + 1) * capacity, :] = picked[
                 expert * capacity : (expert + 1) * capacity
@@ -336,19 +483,22 @@
     lax.fori_loop(0, owned, expert_step, 0)
 
 
-def ring_experts(normed, dispatch, ex_gate, ex_up, ex_down):
-    count = dispatch.shape[0]
-    owned = ex_gate.shape[0]
-    rows = count * dispatch.shape[1] // owned
-    own_rows, width = normed.shape
+def ring_experts(block, top, capacity, ex_gate, ex_up, ex_down):
+    count = lax.axis_size("seq")
+    owned, width = ex_gate.shape[:2]
+    rows = count * capacity
+    own_rows, wide = block.shape
     vmem, far = pl.BlockSpec(memory_space=pltpu.VMEM), pl.BlockSpec(memory_space=pl.ANY)
     return pl.pallas_call(
-        functools.partial(ring_experts_kernel, count),
-        out_shape=jax.ShapeDtypeStruct((owned, rows, width), jnp.bfloat16),
-        in_specs=[vmem, vmem, far, far, far],
-        out_specs=vmem,
+        functools.partial(ring_experts_kernel, count, top, capacity),
+        out_shape=[
+            jax.ShapeDtypeStruct((owned, rows, width), jnp.bfloat16),
+            jax.ShapeDtypeStruct((count, own_rows, owned * capacity), jnp.bfloat16),
+        ],
+        in_specs=[vmem, far, far, far],
+        out_specs=[vmem, vmem],
         scratch_shapes=[
-            pltpu.VMEM((count, own_rows, width), jnp.bfloat16),
+            pltpu.VMEM((count, own_rows, wide), jnp.bfloat16),
             pltpu.VMEM((owned, rows, width), jnp.bfloat16),
             pltpu.VMEM(ex_gate.shape, jnp.bfloat16),
             pltpu.VMEM(ex_up.shape, jnp.bfloat16),
@@ -361,7 +511,7 @@
             collective_id=1, has_side_effects=True, vmem_limit_bytes=48 * 1024 * 1024
         ),
         cost_estimate=pl.CostEstimate(flops=40_000_000_000, bytes_accessed=30_000_000, transcendentals=0),
-    )(normed, dispatch, ex_gate, ex_up, ex_down)
+    )(block, ex_gate, ex_up, ex_down)
 
 
 def ring_sum_kernel(count, outs, combine, tied, total, stage, landed, send_sem, recv_sem):
@@ -372,12 +522,11 @@
     half, piece_rows = width // 2, own_rows // 2
 
     def partial(slot, way, piece):
-        source = ring_seq(lax.rem(place + count - slot, count), count)
         columns = slice(way * half, (way + 1) * half)
         held = jnp.concatenate(
             [outs[e, slot * capacity : (slot + 1) * capacity, columns] for e in range(owned)], axis=0
         )
-        weights = combine[source, piece * piece_rows : (piece + 1) * piece_rows, :]
+        weights = combine[slot, piece * piece_rows : (piece + 1) * piece_rows, :]
         return jnp.dot(weights, held, preferred_element_type=jnp.float32)
 
     flying = {}
@@ -461,25 +610,11 @@
     state_size = in_bc.shape[1] // 2
     local_heads = a_log.shape[0]
     head_width = conv_x.shape[1] // local_heads
-    stream = lax.all_gather(tokens, "exp", axis=0, tiled=True)
-    owned = ex_gate.shape[0]
-    capacity = own_rows * routes.shape[1] * 4 // (3 * owned * seq_count)
-    packed = jnp.concatenate([routes.astype(jnp.float32), gates], axis=1)
-    routing = lax.all_gather(packed, "seq", axis=0, tiled=True)
-    first = jnp.reshape(lax.axis_index("seq") * owned, (1,)).astype(jnp.int32)
-    dispatch, combine = call(
-        functools.partial(route_kernel, seq_count, capacity),
-        [
-            ((seq_count, owned * capacity, own_rows), jnp.bfloat16),
-            ((seq_count, own_rows, owned * capacity), jnp.bfloat16),
-        ],
-        [],
-        1e8,
-        first,
-        routing,
-    )
-    row_count = stream.shape[0]
-    normed_in = rms_rows(stream.astype(jnp.float32), in_gain).astype(jnp.bfloat16)
+    capacity = own_rows * routes.shape[1] * 4 // (3 * ex_gate.shape[0] * seq_count)
+    packed = jnp.concatenate([routes.astype(jnp.bfloat16), gates.astype(jnp.bfloat16)], axis=1)
+    packed = jnp.pad(packed, ((0, 0), (0, LANES - packed.shape[1])))
+    row_count = own_rows * lax.axis_size("exp")
+    normed_in = gather_normed(tokens, in_gain)
     conv_in_x = jnp.dot(normed_in, in_x, preferred_element_type=jnp.float32).astype(jnp.bfloat16)
     conv_in_bc = jnp.dot(normed_in, in_bc, preferred_element_type=jnp.float32).astype(jnp.bfloat16)
     dt_raw = jnp.dot(normed_in, jnp.pad(in_dt, ((0, 0), (0, LANES - local_heads))), preferred_element_type=jnp.float32).astype(jnp.bfloat16)
@@ -566,13 +701,10 @@
         norm_gain[None],
         out_w,
     )
-    mix_sum = lax.psum_scatter(mix_term, "exp", scatter_dimension=0, tiled=True).astype(jnp.float32)
-    row_scale = lax.rsqrt(mix_sum[:, width : width + 1] / DI + epsilon)
-    mixer_out = mix_sum[:, :width] * row_scale
-    residual = tokens.astype(jnp.float32) + mixer_out
-    normed = rms_rows(residual, post_gain).astype(jnp.bfloat16)
+    residual, block = sum_rows(mix_term, tokens, post_gain, packed)
+    normed = block[:, :width]
     normed_all = lax.all_gather(normed, "exp", axis=0, tiled=True)
-    expert_out = ring_experts(normed, dispatch, ex_gate, ex_up, ex_down)
+    expert_out, combine = ring_experts(block, routes.shape[1], capacity, ex_gate, ex_up, ex_down)
     shared_hidden = (
         jax.nn.silu(jnp.dot(normed_all, sh_gate, preferred_element_type=jnp.float32))
         * jnp.dot(normed_all, sh_up, preferred_element_type=jnp.float32)

time: 265 us -> 214 us (0.81)
  waiting for transfers between devices: 74.2 us -> 0.8 us
  Pallas kernels: 93.4 us -> 141 us
  blocking collectives: 35.7 us -> 0 us
  local copies, waits for them, and re-layouts: 11 us -> 19.9 us
    pallas_call x1 -> x3, Pallas kernels: 41.6 us -> 91.5 us  [the longest x1 64.2 us: ring_experts(): pl.pallas_call(functools.partial(ring_experts_kernel, count, top, capacit...]
    all_gather x1 -> x0, blocking collectives: 35.7 us -> none  [body(): routing = lax.all_gather(packed, 'seq', axis=0, tiled=True)]
    reduce_scatter x1 -> x0, waiting for transfers between devices: 28.9 us -> none  [body(): lax.psum_scatter(mix_term, 'exp', scatter_dimension=0, tiled=True)]
    all_gather x1 -> x0, waiting for transfers between devices: 21.8 us -> none  [body(): stream = lax.all_gather(tokens, 'exp', axis=0, tiled=True)]
    reduce_scatter x1, waiting for transfers between devices: 18.6 us -> 0.01 us  [body(): lax.psum_scatter(placed, 'seq', scatter_dimension=0, tiled=True)]
    ppermute x3, waiting for transfers between devices: 4.14 us -> 0.24 us  [from_behind(): return lax.ppermute(block, axis, route)]
    unnamed x58 -> x48, local copies, waits for them, and re-layouts: 10.2 us -> 13 us
    pallas_call x5 -> x4, Pallas kernels: 16.7 us -> 14.6 us  [call(): pl.pallas_call(kernel, out_shape=[jax.ShapeDtypeStruct(s, t) for s, t in...]
  transfers between devices with their start and end apart: 8 -> 6, of which waited for: 6 -> 1; matrix products, arithmetic and copies ran while one was open for 3% -> 11% of each run, Pallas kernels for 33% -> 48%
where the time goes in v3:
time: 214 us; the launch traced here: 212 us
  Pallas kernels  141 us (66%)
  local copies, waits for them, and re-layouts  19.9 us (9%)
  matrix products  15.9 us (7%)
  between operations  15.8 us (7%)
  starting transfers between devices  10.9 us (5%)
  other arithmetic  7.73 us (4%)
    pallas_call x1, Pallas kernels, ring_experts(): pl.pallas_call(functools.partial(ring_experts_kernel, count, top, capacit...  64.2 us
    pallas_call x1, Pallas kernels, ring_sum(): pl.pallas_call(functools.partial(ring_sum_kernel, count), out_shape=jax.S...  35.2 us
    pallas_call x4, Pallas kernels, call(): pl.pallas_call(kernel, out_shape=[jax.ShapeDtypeStruct(s, t) for s, t in...  14.6 us
    pallas_call x1, Pallas kernels, gather_normed(): pl.pallas_call(gather_kernel, out_shape=jax.ShapeDtypeStruct((count * row...  13.9 us
    pallas_call x1, Pallas kernels, sum_rows(): pl.pallas_call(sum_kernel, out_shape=[jax.ShapeDtypeStruct((rows, width),...  13.4 us
    unnamed x48, local copies, waits for them, and re-layouts  13 us
    ppermute x3, starting transfers between devices, from_behind(): return lax.ppermute(block, axis, route)  10.5 us
    dot_general x1, matrix products, body(): jnp.dot(shared_hidden, sh_down, preferred_element_type=jnp.float32)  5.02 us
  transfers between devices with their start and end apart: 6, of which 1 were waited for; matrix products, arithmetic and copies ran while one was open for 11% of the time, Pallas kernels for 48%

profile of v3, /device:TPU:0, one launch (start us, length us, event | category | flops | bytes accessed | tf_op | source)
XLA Modules:
  0.0 212.4 jit_solution(12764449762419303523)
XLA Ops:
  8.0 0.0 copy-start
  8.0 0.0 all-gather.2.cloned.1.call-start
  8.1 0.9 broadcast_in_dim.18.gain
  8.9 1.0 copy-done.5
  9.9 13.9 %shard_map.239 = bf16[512,1536]{1,0:T(8,128)(2,1)S(1)} custom-call(bf16[128,1536]{1,0:T(8,128)(2,1)S(1)} %copy-done.5, f32[1,1536]{1,0:T(1,128)S(1)} %broadcast_in_dim.18.gain), custom_call_target="tpu_custom_call" | custom-call | tf_op jit(solution)/shard_map/pallas_call | solution.py:277
  23.8 0.0 copy-done.22
  23.9 0.0 copy-start.2
  23.9 0.6 convolution_convert_fusion.3.bcin
  24.5 0.0 copy-start.23
  24.5 0.0 copy-start.19
  24.5 0.0 copy-start.20
  24.5 1.4 convolution_convert_fusion.2.xin
  25.9 0.6 pad_maximum_fusion.1
  26.5 4.0 %collective-permute-start = (bf16[16,1024]{1,0:T(8,128)(2,1)}, bf16[16,1024]{1,0:T(8,128)(2,1)}, u32[]{:S(2)}, u32[]{:S(2)}) collective-permute-start(bf16[16,1024]{1,0:T(8,128)(2,1)} %pad_maximum_fusion.1), channel_id=1, source_target_pairs={{0,4},{4,8},{8,12},{12,16},{16,20},{20,24},{24,28},{1,5},{5,9},{9,... | collective-permute-start | bytes 98312 | tf_op jit(solution)/shard_map/ppermute | solution.py:19
  30.5 0.5 pad_bitcast_fusion.d_skip
  31.0 0.0 copy-done.20
  31.0 2.0 convolution_convert_fusion.4.dt_raw
  33.0 0.0 copy-start.21
  33.0 0.0 copy-start.11
  33.0 4.0 %convolution_convert_fusion.1.gate_raw = bf16[512,768]{1,0:T(8,128)(2,1)} fusion(bf16[512,1536]{1,0:T(8,128)(2,1)S(1)} %copy-done.3, bf16[1536,768]{1,0:T(8,128)(2,1)} %param.26), kind=kOutput, calls=%fused_computation.1 | convolution fusion | flops 1208352768 | bytes 4718592 | tf_op jit(solution)/shard_map/dot_general | solution.py:623
  37.0 1.3 reduce-window.9
  38.3 0.0 copy-done.21
  38.3 1.2 pad_bitcast_fusion.1
  39.6 0.6 pad_maximum_fusion.2
  40.2 1.3 pad_add_fusion.meta
  41.5 0.7 broadcast_in_dim.22.gain
  42.2 0.7 broadcast_in_dim.23.gain
  42.9 1.4 copy.28
  44.3 0.8 pad.22.packed
  45.0 0.0 collective-permute-done.edge
  45.1 0.0 copy-start.10
  45.1 0.7 copy-done.10
  45.8 0.7 copy-done.12
  46.4 0.7 copy-done.13
  47.1 0.6 copy-done.14
  47.7 5.9 %shard_map.240 = (bf16[512,768]{1,0:T(8,128)(2,1)S(1)}, bf16[512,256]{1,0:T(8,128)(2,1)S(1)}, bf16[512,768]{1,0:T(8,128)(2,1)S(1)}, bf16[768,512]{1,0:T(8,128)(2...) custom-call(s32[17]{0:T(128)S(1)} %copy-done.12, ...), custom_call_target="tpu_custom_call" | custom-call | flops 300000000 | bytes 1229892 | tf_op jit(solution)/shard_map/pallas_call | solution.py:34
  53.6 2.9 %collective-permute-start.2 = (bf16[784,128]{1,0:T(8,128)(2,1)S(1)}, bf16[784,128]{1,0:T(8,128)(2,1)S(1)}, u32[]{:S(2)}, u32[]{:S(2)}) collective-permute-start(bf16[784,128]{1,0:T(8,128)(2,1)S(1)} %get-tuple-element.22), channel_id=1, source_target_pairs={{0,8},{4,12},{8,16},{12,20},{16,24},{20,28},{1,9},{5,13},{9,17},{1... | collective-permute-start | bytes 602120 | tf_op jit(solution)/shard_map/ppermute | solution.py:19
  56.5 3.6 %collective-permute-start.1 = (bf16[784,128]{1,0:T(8,128)(2,1)S(1)}, bf16[784,128]{1,0:T(8,128)(2,1)S(1)}, u32[]{:S(2)}, u32[]{:S(2)}) collective-permute-start(bf16[784,128]{1,0:T(8,128)(2,1)S(1)} %get-tuple-element.22), channel_id=1, source_target_pairs={{0,4},{4,8},{8,12},{12,16},{16,20},{20,24},{24,28},{1,5},{5,9},{9,... | collective-permute-start | bytes 602120 | tf_op jit(solution)/shard_map/ppermute | solution.py:19
  60.2 0.6 copy-done.15
  60.7 3.3 %shard_map.241.mixed = f32[512,768]{1,0:T(8,128)S(1)} custom-call(s32[17]{0:T(128)S(1)} %copy-done.12, bf16[512,256]{1,0:T(8,128)(2,1)S(1)} %get-tuple-element.16.bc, bf16[512,768]{1,0:T(8,128)(2,1)S(1)} %get-tuple-element.17.xc, bf16[512,768]{1,0:T(8,128)(2,1)S(1)} %get-tuple-element.18.drive, f32[512,128]{1,0:T(8,128)S(1)} %get-tuple-element.19.cum, ...), custom_call_target="tpu_custom_call" | custom-call | flops 3000000000 | bytes 2359876 | tf_op jit(solution)/shard_map/pallas_call | solution.py:34
  64.1 0.0 collective-permute-done.2
  64.1 0.2 collective-permute-done.1
  64.4 1.3 shard_map.242
  65.6 1.2 copy-done.1
  66.8 4.2 %shard_map.243.term = bf16[512,1664]{1,0:T(8,128)(2,1)S(1)} custom-call(f32[512,768]{1,0:T(8,128)S(1)} %shard_map.241.mixed, bf16[512,768]{1,0:T(8,128)(2,1)S(1)} %copy-done.16, bf16[512,256]{1,0:T(8,128)(2,1)S(1)} %get-tuple-element.16.bc, bf16[768,128]{1,0:T(8,128)(2,1)S(1)} %get-tuple-element.23.state_in, f32[512,128]{1,0:T(8,128)S(1)} %get-tuple-element.24.lead, ...), custom_call_target="tpu_custom_call" | custom-call | flops 3000000000 | bytes 5442560 | tf_op jit(solution)/shard_map/pallas_call | solution.py:34
  71.0 13.4 %shard_map.244 = (f32[128,1536]{1,0:T(8,128)S(1)}, bf16[128,1664]{1,0:T(8,128)(2,1)S(1)}) custom-call(bf16[512,1664]{1,0:T(8,128)(2,1)S(1)} %shard_map.243.term, bf16[128,1536]{1,0:T(8,128)(2,1)S(1)} %copy-done.6, f32[1,1536]{1,0:T(1,128)S(1)} %broadcast_in_dim.23.gain, bf16[128,128]{1,0:T(8,128)(2,1)S(1)} %pad.22.packed), custom_call_target="tpu_custom_call" | custom-call | tf_op jit(solution)/shard_map/pallas_call | solution.py:350
  84.4 0.8 slice.11
  85.2 0.8 copy-done.8
  85.9 0.0 all-gather.2.cloned.1.call-update
  85.9 0.0 reduce-scatter.5.cloned.1.call-start
  86.0 0.5 reduce-scatter.5.cloned.1.call-update
  86.5 0.3 reduce-scatter.3.cloned.1.call-start
  86.8 1.0 copy-done.9
  87.8 64.2 %shard_map.245 = (bf16[4,256,1536]{2,1,0:T(8,128)(2,1)S(1)}, bf16[8,128,128]{2,1,0:T(8,128)(2,1)S(1)}) custom-call(bf16[128,1664]{1,0:T(8,128)(2,1)S(1)} %copy-done.9, bf16[4,1536,512]{2,1,0:T(8,128)(2,1)} %gate_hbm.1, bf16[4,1536,512]{2,1,0:T(8,128)(2,1)} %up_hbm.1, bf16[4,512,1536]{2,1,0:T(8,128)(2,1)} %down_hbm.1), custom_call_target="tpu_custom_call" | custom-call | flops 40000000000 | bytes 30000000 | tf_op jit(solution)/shard_map/pallas_call | solution.py:492
  152.0 1.6 copy-done.17
  153.6 3.0 %fusion.10 = f32[512,256]{1,0:T(8,128)} fusion(bf16[512,1536]{1,0:T(8,128)(2,1)} %all-gather.2.cloned.1.call-done, bf16[1536,256]{1,0:T(8,128)(2,1)} %param.38), kind=kOutput, calls=%fused_computation.24 | convolution fusion | flops 402653184 | bytes 2883584 | tf_op jit(solution)/shard_map/dot_general | solution.py:709
  156.6 5.0 %convolution_convert_fusion.tied = bf16[512,1536]{1,0:T(8,128)(2,1)} fusion(bf16[256,1536]{1,0:T(8,128)(2,1)} %param.40, bf16[512,1536]{1,0:T(8,128)(2,1)} %all-gather.2.cloned.1.call-done, bf16[1536,256]{1,0:T(8,128)(2,1)} %param.39, f32[512,256]{1,0:T(8,128)} %fusion.10), kind=kOutput, calls=%fused_computation | convolution fusion | flops 806879232 | bytes 5242880 | tf_op jit(solution)/shard_map/dot_general | solution.py:712
  161.7 0.0 reduce-scatter.3.cloned.1.call-update
  161.7 1.4 copy-done.4
  163.1 1.9 copy-done.18
  165.0 35.2 %shard_map.246 = f32[128,1536]{1,0:T(8,128)S(1)} custom-call(bf16[4,256,1536]{2,1,0:T(8,128)(2,1)S(1)} %copy-done.18, bf16[8,128,128]{2,1,0:T(8,128)(2,1)S(1)} %get-tuple-element.28.combine, bf16[512,1536]{1,0:T(8,128)(2,1)S(1)} %copy-done.4), custom_call_target="tpu_custom_call" | custom-call | flops 40000000000 | bytes 10000000 | tf_op jit(solution)/shard_map/pallas_call | solution.py:563
  200.2 0.9 copy-done.7
  201.1 1.7 convert.1
  202.8 2.1 add_convert_fusion
  (32 shorter events, 0.1 us)
Async XLA Ops:
  8.0 16.5 %copy-start = (bf16[1536,768]{1,0:T(8,128)(2,1)S(1)}, bf16[1536,768]{1,0:T(8,128)(2,1)}, u32[]{:S(2)}) copy-start(bf16[1536,768]{1,0:T(8,128)(2,1)} %param.27) | copy-start | bytes 7077892
  8.0 145.6 %all-gather.2.cloned.1.call-start = ((), (), s32[]{:S(2)}) async-start(), calls=%async_computation.2 | async-start | bytes 1966080 | tf_op jit(solution)/shard_map/all_gather | solution.py:706
  8.9 1.0 copy-start.5
  9.9 13.9 %copy-start.22 = (bf16[1536,256]{1,0:T(8,128)(2,1)S(1)}, bf16[1536,256]{1,0:T(8,128)(2,1)}, u32[]{:S(2)}) copy-start(bf16[1536,256]{1,0:T(8,128)(2,1)} %param.28) | copy-start | bytes 2359300
  23.9 2.0 copy-start.2
  24.5 6.1 %copy-start.23 = (f32[12]{0:T(128)S(1)}, f32[12]{0:T(128)}, u32[]{:S(2)}) copy-start(f32[12]{0:T(128)} %param.34) | copy-start | bytes 148
  24.5 6.5 %copy-start.19 = (s32[128,6]{0,1:T(8,128)S(1)}, s32[128,6]{0,1:T(8,128)}, u32[]{:S(2)}) copy-start(s32[128,6]{0,1:T(8,128)} %param.44) | copy-start | bytes 9220
  24.5 6.5 %copy-start.20 = (f32[128,6]{0,1:T(8,128)S(1)}, f32[128,6]{0,1:T(8,128)}, u32[]{:S(2)}) copy-start(f32[128,6]{0,1:T(8,128)} %param.45) | copy-start | bytes 9220
  26.5 18.5 %collective-permute-start = (bf16[16,1024]{1,0:T(8,128)(2,1)}, bf16[16,1024]{1,0:T(8,128)(2,1)}, u32[]{:S(2)}, u32[]{:S(2)}) collective-permute-start(bf16[16,1024]{1,0:T(8,128)(2,1)} %pad_maximum_fusion.1), channel_id=1, source_target_pairs={{0,4},{4,8},{8,12},{12,16},{16,20},{20,24},{24,28},{1,5},{5,9},{9,... | collective-permute-start | bytes 98312 | tf_op jit(solution)/shard_map/ppermute | solution.py:19
  30.5 2.5 %copy-start.3 = (bf16[512,1536]{1,0:T(8,128)(2,1)S(1)}, bf16[512,1536]{1,0:T(8,128)(2,1)}, u32[]{:S(2)}) copy-start(bf16[512,1536]{1,0:T(8,128)(2,1)} %copy-done.2) | copy-start | bytes 4718596
  33.0 5.3 %copy-start.21 = (f32[12]{0:T(128)S(1)}, f32[12]{0:T(128)}, u32[]{:S(2)}) copy-start(f32[12]{0:T(128)} %param.33) | copy-start | bytes 148
  33.0 12.0 %copy-start.11 = (f32[4,256]{1,0:T(4,128)S(1)}, f32[4,256]{1,0:T(4,128)}, u32[]{:S(2)}) copy-start(f32[4,256]{1,0:T(4,128)} %conv_bc.1) | copy-start | bytes 12292
  45.1 0.7 copy-start.10
  45.8 0.7 copy-start.12
  46.4 0.7 copy-start.13
  47.1 0.6 copy-start.14
  53.6 10.5 %collective-permute-start.2 = (bf16[784,128]{1,0:T(8,128)(2,1)S(1)}, bf16[784,128]{1,0:T(8,128)(2,1)S(1)}, u32[]{:S(2)}, u32[]{:S(2)}) collective-permute-start(bf16[784,128]{1,0:T(8,128)(2,1)S(1)} %get-tuple-element.22), channel_id=1, source_target_pairs={{0,8},{4,12},{8,16},{12,20},{16,24},{20,28},{1,9},{5,13},{9,17},{1... | collective-permute-start | bytes 602120 | tf_op jit(solution)/shard_map/ppermute | solution.py:19
  56.5 7.8 %collective-permute-start.1 = (bf16[784,128]{1,0:T(8,128)(2,1)S(1)}, bf16[784,128]{1,0:T(8,128)(2,1)S(1)}, u32[]{:S(2)}, u32[]{:S(2)}) collective-permute-start(bf16[784,128]{1,0:T(8,128)(2,1)S(1)} %get-tuple-element.22), channel_id=1, source_target_pairs={{0,4},{4,8},{8,12},{12,16},{16,20},{20,24},{24,28},{1,5},{5,9},{9,... | collective-permute-start | bytes 602120 | tf_op jit(solution)/shard_map/ppermute | solution.py:19
  60.1 0.6 copy-start.15
  64.4 2.4 %copy-start.16 = (bf16[512,768]{1,0:T(8,128)(2,1)S(1)}, bf16[512,768]{1,0:T(8,128)(2,1)}, u32[]{:S(2)}) copy-start(bf16[512,768]{1,0:T(8,128)(2,1)} %convolution_convert_fusion.1.gate_raw) | copy-start | bytes 2359300
  65.6 1.2 copy-start.1
  66.8 4.2 %copy-start.6 = (bf16[128,1536]{1,0:T(8,128)(2,1)S(1)}, bf16[128,1536]{1,0:T(8,128)(2,1)}, u32[]{:S(2)}) copy-start(bf16[128,1536]{1,0:T(8,128)(2,1)} %tokens.3) | copy-start | bytes 1179652
  85.2 0.8 copy-start.8
  85.9 115.2 %reduce-scatter.5.cloned.1.call-start = ((), (), s32[]{:S(2)}) async-start(), calls=%async_computation.4 | async-start | bytes 1769472 | tf_op jit(solution)/shard_map/reduce_scatter | solution.py:687
  86.5 116.3 %reduce-scatter.3.cloned.1.call-start = ((), (), s32[]{:S(2)}) async-start(), calls=%async_computation.3 | async-start | bytes 1966080 | tf_op jit(solution)/shard_map/reduce_scatter | solution.py:713
  86.8 1.0 copy-start.9
  152.0 1.6 copy-start.17
  161.7 1.4 copy-start.4
  163.1 1.9 copy-start.18
  200.2 0.9 copy-start.7
Sparse Core Ops, SparseCore 0:
  86.1 22.1 all-gather.1
Sparse Core Ops, SparseCore 1:
  89.8 72.2 reduce-scatter.4
  164.6 27.0 reduce-scatter.2
